TPU v7x, 32 devices: a whole 2x2x4 slice. The times are simulated.
32 devices in a mesh: wide: 8 (over z, y), pair: 4 (over x, core).
Axes of the slice: x: 2, y: 2, z: 4, core: 2. Of those that a mesh axis runs over, the one named last changes fastest.
Arguments:
- blocks: bfloat16 [128, 1024, 512], P('pair', 'wide'), may hold values from -6 to 6
- basis_a: bfloat16 [1024, 64], replicated, may hold values from -0.1875 to 0.1875
- basis_b: bfloat16 [512, 64], replicated, may hold values from -0.25 to 0.25
- sketch: bfloat16 [128, 64], P(('pair', 'wide')), may hold values from -6 to 6
Outputs:
- transfer: float32 [4096, 64], P(('wide', 'pair'))
- coefficients: float32 [128, 64], P(('pair', 'wide'))
All inputs are finite; a program needn't handle non-finite values.
Results may differ from a plain program's by a relative error of at most 0.0041.
Values may be sent and summed in bfloat16 or wider, within the bound.
No kernel may reach another device: no remote copies, remote signals or barrier semaphores. Data moves between devices by JAX's collectives and lax.ppermute only.
A program may use at most 64 MiB of HBM per device.

v0:
```python
import jax
import jax.numpy as jnp
from jax import lax
from jax.sharding import PartitionSpec as P


def orthonormal(sketched, gram):
    lower = jnp.linalg.cholesky(gram)
    return lax.linalg.triangular_solve(
        lower, sketched, left_side=False, lower=True, transpose_a=True
    )


def per_device(blocks, basis_a, basis_b, sketch):
    fibres = sketch.shape[0]
    rank_a = basis_a.shape[1]
    rank_b = basis_b.shape[1]
    narrowed = jnp.einsum(
        "fac,cr->far", blocks, basis_b, preferred_element_type=jnp.float32
    ).astype(jnp.bfloat16)
    regrouped = lax.all_to_all(narrowed, "wide", split_axis=0, concat_axis=1, tiled=True)
    projected = jnp.einsum(
        "ap,far->fpr", basis_a, regrouped, preferred_element_type=jnp.float32
    ).astype(jnp.bfloat16)
    projected = projected.reshape(fibres, rank_a * rank_b)
    partial_value = jnp.einsum("fj,fk->jk", projected, sketch, preferred_element_type=jnp.float32)
    own_count = rank_a * rank_b // lax.axis_size(("wide", "pair"))
    sketch_all = lax.psum(partial_value, ("wide", "pair"))
    gram_matrix = jnp.dot(sketch_all.T, sketch_all, precision=lax.Precision.HIGHEST)
    parent_basis = orthonormal(sketch_all, gram_matrix)
    first_row = lax.axis_index(("wide", "pair")) * own_count
    own_basis = lax.dynamic_slice_in_dim(parent_basis, first_row, own_count, 0)
    transfer = own_basis * jnp.sqrt(jnp.float32(rank_a * rank_b))
    coefficients = jnp.dot(
        projected.astype(jnp.float32), parent_basis, precision=lax.Precision.HIGHEST
    )
    return (transfer, coefficients)


def solution(mesh):
    placed = (P("pair", "wide", None), P(), P(), P(("pair", "wide"), None))
    return jax.shard_map(
        per_device,
        mesh=mesh,
        in_specs=placed,
        out_specs=(P(("wide", "pair"), None), P(("pair", "wide"), None)),
        check_vma=False,
    )
```

profile of v0, /device:TPU:0, one launch (start us, length us, event | category | flops | bytes accessed | tf_op | source)
XLA Modules:
  0.0 189.0 jit_solution(6678659559795567274)
XLA Ops:
  7.2 0.0 copy-start
  7.2 0.0 copy-start.1
  7.2 0.0 all-reduce.2.cloned.1.call-start
  7.2 3.6 %convolution_convert_fusion = bf16[32,128,64]{1,2,0:T(8,128)(2,1)S(1)} fusion(bf16[32,128,512]{2,1,0:T(8,128)(2,1)} %param.4, bf16[512,64]{0,1:T(8,128)(2,1)} %param.6), kind=kOutput, calls=%fused_computation | convolution fusion | flops 268697600 | bytes 4784128 | tf_op jit(solution)/shard_map/fac,cr->far/dot_general | solution.py:18
  10.8 21.6 %all_to_all.18 = bf16[32,128,64]{1,2,0:T(8,128)(2,1)S(1)} all-to-all(bf16[32,128,64]{1,2,0:T(8,128)(2,1)S(1)} %convolution_convert_fusion), channel_id=1, replica_groups=mesh['wide'=8,'pair'=4] {'wide'}, dimensions={0} | all-to-all | bytes 1048576 | tf_op jit(solution)/shard_map/all_to_all | solution.py:21
  32.4 0.0 copy-done
  32.4 0.3 fusion
  32.7 0.1 copy.9
  32.8 0.1 reshape.16
  32.9 0.0 copy-done.1
  32.9 1.4 fusion.9
  34.3 0.0 all-reduce.2.cloned.1.call-update
  34.4 129.1 %all-reduce.2.cloned.1.call-done = f32[4096,64]{0,1:T(8,128)} async-done(((f32[4096,64]{0,1:T(8,128)}), f32[4096,64]{0,1:T(8,128)}) %all-reduce.2.cloned.1.call-update) | async-done | bytes 1048592 | tf_op jit(solution)/shard_map/psum | solution.py:28
  163.4 2.5 %fusion.10 = f32[64,64]{1,0:T(8,128)S(1)} fusion(f32[4096,64]{0,1:T(8,128)} %all-reduce.2.cloned.1.call-done), kind=kOutput, calls=%fused_computation.19 | convolution fusion | flops 201326592 | bytes 1064960 | tf_op jit(solution)/shard_map/dot_general | solution.py:29
  165.9 0.1 copy.10
  166.0 5.8 %cholesky.16 = f32[64,64]{1,0:T(8,128)S(1)} custom-call(f32[64,64]{1,0:T(8,128)S(1)} %fusion.8), custom_call_target="Cholesky" | custom-call | tf_op jit(solution)/shard_map/jit(cholesky)/cholesky | solution.py:8
  171.9 0.6 compare_reduce_fusion
  172.6 0.7 fusion.5
  173.2 4.9 %custom-call.6 = f32[1,64,64]{1,2,0:T(8,128)S(1)} custom-call(f32[1,64,64]{2,1,0:T(8,128)S(1)} %fusion.5), custom_call_target="InvertDiagBlocksLowerTriangular" | custom-call | tf_op jit(solution)/shard_map/triangular_solve | solution.py:9
  178.1 2.3 %fusion.6 = f32[4096,64]{0,1:T(8,128)S(1)} fusion(f32[4096,64]{0,1:T(8,128)} %all-reduce.2.cloned.1.call-done, f32[1,64,64]{1,2,0:T(8,128)S(1)} %custom-call.6), kind=kOutput, calls=%fused_computation.9 | convolution fusion | flops 201326592 | bytes 2113536 | tf_op jit(solution)/shard_map/triangular_solve | solution.py:9
  180.4 1.2 fusion.11
  181.6 0.6 dynamic-slice_multiply_fusion
  (2 shorter events, 0.0 us)
Async XLA Ops:
  7.2 25.3 %copy-start = (bf16[1024,64]{0,1:T(8,128)(2,1)S(1)}, bf16[1024,64]{0,1:T(8,128)(2,1)}, u32[]{:S(2)}) copy-start(bf16[1024,64]{0,1:T(8,128)(2,1)} %param.5) | copy-start | bytes 393220
  7.2 25.8 %copy-start.1 = (bf16[4,64]{1,0:T(4,128)(2,1)S(1)}, bf16[4,64]{1,0:T(4,128)(2,1)}, u32[]{:S(2)}) copy-start(bf16[4,64]{1,0:T(4,128)(2,1)} %param.7) | copy-start | bytes 1540
  7.2 156.2 %all-reduce.2.cloned.1.call-start = ((), (), s32[]{:S(2)}) async-start(), calls=%async_computation.1 | async-start | bytes 2097152 | tf_op jit(solution)/shard_map/psum | solution.py:28
Sparse Core Ops, SparseCore 0:
  34.5 128.8 all-reduce.1
where the time goes:
time: 189 us
  waiting for transfers between devices  129 us (68%)
  blocking collectives  21.6 us (11%)
  between operations  14.1 us (7%)
  other arithmetic  12.7 us (7%)
  matrix products  11.2 us (6%)
    psum x1, waiting for transfers between devices, per_device(): sketch_all = lax.psum(partial_value, ('wide', 'pair'))  129 us
    all_to_all x1, blocking collectives, per_device(): lax.all_to_all(narrowed, 'wide', split_axis=0, concat_axis=1, tiled=True)  21.6 us
    another operation x3, other arithmetic, orthonormal(): lower = jnp.linalg.cholesky(gram)  6.52 us
    another operation x2, other arithmetic, orthonormal(): lax.linalg.triangular_solve(lower, sketched, left_side=False, lower=True,...  5.55 us
  transfers between devices with their start and end apart: 1, of which 1 were waited for; matrix products, arithmetic and copies ran while one was open for 0% of the time, Pallas kernels for 0%

commit v1 on v0

v1 whole, which is shorter than its diff:
```python
import functools

import jax
import jax.numpy as jnp
from jax import lax
from jax.experimental import pallas as pl
from jax.experimental.pallas import tpu as pltpu
from jax.sharding import PartitionSpec as P

F32 = jnp.float32
BF16 = jnp.bfloat16
LANES = 128
SQUARE = 4
CHUNKS = 4
NT = (((1,), (1,)), ((), ()))


def split3(x):
    high = x.astype(BF16)
    rest = x - high.astype(F32)
    middle = rest.astype(BF16)
    low = (rest - middle.astype(F32)).astype(BF16)
    return high, middle, low


def project_kernel(blocks, basis_a, basis_b, sketch, *refs):
    outs = refs[:SQUARE]
    held, rows_a, held_b, held_s, diagonal, wanted, sums, sems = refs[SQUARE:]
    wide = lax.axis_index("wide")
    fibres, rows, columns = blocks.shape
    rank_b = basis_b.shape[1]
    rank_a = basis_a.shape[1]
    pairs = fibres // 2
    quad = 4 * rank_b
    per_chunk = fibres // CHUNKS
    copies = [
        pltpu.make_async_copy(basis_b, held_b, sems.at[CHUNKS]),
        pltpu.make_async_copy(
            basis_a.at[pl.ds(pl.multiple_of(wide * rows, rows), rows), :], rows_a, sems.at[CHUNKS + 1]
        ),
        pltpu.make_async_copy(sketch, held_s, sems.at[CHUNKS + 2]),
    ]
    for c in range(CHUNKS):
        part = pl.ds(c * per_chunk, per_chunk)
        copies.append(pltpu.make_async_copy(blocks.at[part], held.at[part], sems.at[c]))
    for copy in copies:
        copy.start()
    diagonal[...] = jnp.zeros(diagonal.shape, BF16)
    copies[0].wait()
    basis = held_b[...]
    for j in range(4):
        part = [jnp.zeros((columns, LANES), BF16)] * (quad // LANES)
        empty = jnp.zeros((columns, rank_b), BF16)
        both = [basis, empty] if j % 2 == 0 else [empty, basis]
        part[j // 2] = jnp.concatenate(both, axis=1)
        diagonal[pl.ds(j * columns, columns), pl.ds(j // 2 * LANES, LANES)] = part[j // 2]
    copies[1].wait()
    turned = rows_a[...].astype(F32).T
    wanted[...] = turned.reshape(wanted.shape)
    square = lax.rem(wide, SQUARE)
    halves = wanted.shape[0]
    left = jnp.concatenate(
        [wanted[half, square ^ k] for k in range(SQUARE) for half in range(halves)], axis=0
    ).astype(BF16)
    for c in range(CHUNKS):
        copies[3 + c].wait()
        here = held[pl.ds(c * per_chunk, per_chunk)]
        here = here.reshape(per_chunk // 4, 4, rows, columns)
        lhs = jnp.concatenate([here[:, j].reshape(per_chunk // 4 * rows, columns) for j in range(4)], axis=1)
        narrowed = jnp.dot(lhs, diagonal[...], preferred_element_type=F32).astype(BF16)
        for q in range(per_chunk // 4):
            found = jnp.dot(left, narrowed[q * rows : (q + 1) * rows], preferred_element_type=F32)
            for t in range(quad // LANES):
                s = (c * per_chunk // 4 + q) * 2 + t
                sums[pl.ds(s, rank_a, stride=pairs), :] = found[:, t * LANES : (t + 1) * LANES]
    copies[2].wait()
    mine = held_s[...].astype(F32)
    own = mine.shape[0]
    row = lax.broadcasted_iota(jnp.int32, (pairs, LANES), 0)
    tile = jnp.zeros((pairs, LANES), F32)
    for j in range(own // 2):
        line = jnp.concatenate([mine[2 * j : 2 * j + 1], mine[2 * j + 1 : 2 * j + 2]], axis=1)
        tile = jnp.where(row == wide * (own // 2) + j, line, tile)
    count = rank_a // SQUARE
    for k in range(SQUARE):
        found = sums[pl.ds(k * count * pairs, count * pairs), :].reshape(count, pairs, LANES)
        outs[k][pl.ds(0, count)] = found.astype(BF16)
        outs[k][count] = tile.astype(BF16)


def project(blocks, basis_a, basis_b, sketch):
    fibres, rows, columns = blocks.shape
    rank_a = basis_a.shape[1]
    rank_b = basis_b.shape[1]
    pairs = fibres // 2
    wide = lax.axis_size("wide")
    count = rank_a // SQUARE
    out = jax.ShapeDtypeStruct((count + 1, pairs, LANES), BF16)
    vmem = pl.BlockSpec(memory_space=pltpu.VMEM)
    anywhere = pl.BlockSpec(memory_space=pl.ANY)
    return pl.pallas_call(
        project_kernel,
        out_shape=[out] * SQUARE,
        in_specs=[anywhere] * 4,
        out_specs=[vmem] * SQUARE,
        scratch_shapes=[
            pltpu.VMEM(blocks.shape, BF16),
            pltpu.VMEM((rows, rank_a), BF16),
            pltpu.VMEM(basis_b.shape, BF16),
            pltpu.VMEM(sketch.shape, BF16),
            pltpu.VMEM((4 * columns, 4 * rank_b), BF16),
            pltpu.VMEM((wide // SQUARE, SQUARE, rank_a // wide, rows), F32),
            pltpu.VMEM((rank_a * pairs, LANES), F32),
            pltpu.SemaphoreType.DMA((CHUNKS + 3,)),
        ],
        compiler_params=pltpu.CompilerParams(vmem_limit_bytes=32 * 2**20),
        name="project",
    )(blocks, basis_a, basis_b, sketch)


def square_kernel(gathered, moment, own, turned_sketch, held):
    groups, tiles, pairs, _ = gathered.shape
    count = tiles - 1
    rank = LANES // 2
    wide = lax.axis_index("wide")
    pair = lax.axis_index("pair")

    def tile(p):
        return gathered[:, p].reshape(groups * pairs, LANES)

    parts = []
    for m in range(count // 2):
        even, odd = tile(2 * m), tile(2 * m + 1)
        first = jnp.concatenate([even[:, :rank], odd[:, :rank]], axis=1)
        second = jnp.concatenate([even[:, rank:], odd[:, rank:]], axis=1)
        parts.append(jnp.concatenate([first, second], axis=0))
    projected = jnp.concatenate(parts, axis=1)
    rides = tile(count).astype(F32)
    omega = jnp.concatenate([rides[:, :rank], rides[:, rank:]], axis=0).T.astype(BF16)
    turned_sketch[...] = omega
    sketched = jnp.dot(omega, projected, preferred_element_type=F32)
    terms = jnp.concatenate(split3(sketched), axis=0)
    product = lax.dot_general(terms, projected, NT, preferred_element_type=F32)
    columns = omega.shape[0]
    moment[...] = product[:columns] + (product[columns : 2 * columns] + product[2 * columns :])
    for m in range(count // 2):
        held[m] = sketched[:, m * LANES : (m + 1) * LANES]
    own[...] = held[lax.div(wide, SQUARE) * groups + pair]


def square_product(gathered):
    groups, tiles, pairs, _ = gathered.shape
    rank = LANES // 2
    vmem = pl.BlockSpec(memory_space=pltpu.VMEM)
    whole = jax.ShapeDtypeStruct((rank, LANES), F32)
    return pl.pallas_call(
        square_kernel,
        out_shape=[whole, whole, jax.ShapeDtypeStruct((rank, LANES), BF16)],
        in_specs=[vmem],
        out_specs=[vmem] * 3,
        scratch_shapes=[pltpu.VMEM(((tiles - 1) // 2, rank, LANES), F32)],
        compiler_params=pltpu.CompilerParams(vmem_limit_bytes=32 * 2**20),
        name="square_product",
    )(gathered)


def finish_kernel(scale, m0, m1, m2, m3, own, turned_sketch, transfer, coefficients):
    wide = lax.axis_index("wide")
    pair = lax.axis_index("pair")
    moment = (m0[...] + m1[...]) + (m2[...] + m3[...])
    rank, fibres = moment.shape
    terms = jnp.concatenate(split3(moment), axis=0)
    product = lax.dot_general(terms, turned_sketch[...], NT, preferred_element_type=F32)
    gram = product[:rank] + (product[rank : 2 * rank] + product[2 * rank :])
    row = lax.broadcasted_iota(jnp.int32, (rank, rank), 0)
    column = lax.broadcasted_iota(jnp.int32, (rank, rank), 1)
    table = jnp.concatenate([gram, (row == column).astype(F32)], axis=1)
    below = lax.broadcasted_iota(jnp.int32, (8, LANES), 0)
    blocks = [table[8 * b : 8 * b + 8] for b in range(rank // 8)]
    inverse = []
    for j in range(rank):
        b, i = divmod(j, 8)
        line = blocks[b][i : i + 1]
        pivot = line[:, j : j + 1]
        inverse.append(line[:, rank:] * lax.rsqrt(pivot))
        line = line / pivot
        for c in range(b, rank // 8):
            factor = blocks[c][:, j : j + 1]
            if c == b:
                factor = jnp.where(below[:, :1] > i, factor, 0.0)
            blocks[c] = blocks[c] - factor * line
    inverse = jnp.concatenate(inverse, axis=0)
    transfer[...] = scale * lax.dot_general(
        own[...].T, inverse, NT, preferred_element_type=F32, precision=lax.Precision.HIGHEST
    )
    count = coefficients.shape[0]
    groups = lax.axis_size("pair")
    per_group = fibres // groups // 2
    j = lax.broadcasted_iota(jnp.int32, (8, fibres), 0)
    at = lax.rem(j, 2) * (fibres // 2) + pair * per_group + wide * (count // 2) + lax.div(j, 2)
    pick = (lax.broadcasted_iota(jnp.int32, (8, fibres), 1) == at).astype(F32)
    mine = lax.dot_general(pick, moment, NT, preferred_element_type=F32, precision=lax.Precision.HIGHEST)
    found = lax.dot_general(mine, inverse, NT, preferred_element_type=F32, precision=lax.Precision.HIGHEST)
    coefficients[...] = found[:count]


def finish(moments, own, turned_sketch, scale, count):
    rank = own.shape[0]
    vmem = pl.BlockSpec(memory_space=pltpu.VMEM)
    return pl.pallas_call(
        functools.partial(finish_kernel, scale),
        out_shape=[
            jax.ShapeDtypeStruct((own.shape[1], rank), F32),
            jax.ShapeDtypeStruct((count, rank), F32),
        ],
        in_specs=[vmem] * 6,
        out_specs=[vmem] * 2,
        compiler_params=pltpu.CompilerParams(vmem_limit_bytes=32 * 2**20),
        name="finish",
    )(*moments, own, turned_sketch)


def partner(x, k):
    return lax.ppermute(x, "wide", [(i, i ^ k) for i in range(lax.axis_size("wide"))])


def in_squares(blocks, basis_a, basis_b, sketch):
    outs = project(blocks, basis_a, basis_b, sketch)
    got = [partner(outs[k], k) for k in range(1, SQUARE)]
    total = outs[0].astype(F32)
    for term in got:
        total = total + term.astype(F32)
    total = total.astype(BF16)
    other = partner(total, SQUARE)
    total = (total.astype(F32) + other.astype(F32)).astype(BF16)
    gathered = lax.all_gather(total, "pair")
    moment, own, turned_sketch = square_product(gathered)
    moments = [moment] + [partner(moment, k) for k in range(1, SQUARE)]
    scale = float((basis_a.shape[1] * basis_b.shape[1]) ** 0.5)
    return tuple(finish(moments, own, turned_sketch, scale, sketch.shape[0]))


def by_columns(blocks, basis_a, basis_b, sketch):
    rank_a, rank_b = basis_a.shape[1], basis_b.shape[1]
    rows = blocks.shape[1]
    wide, pair = lax.axis_size("wide"), lax.axis_size("pair")
    narrowed = jnp.einsum("fac,cr->far", blocks, basis_b, preferred_element_type=F32).astype(BF16)
    own_rows = lax.dynamic_slice_in_dim(basis_a, lax.axis_index("wide") * rows, rows, 0)
    part = jnp.einsum("ap,far->fpr", own_rows, narrowed, preferred_element_type=F32).astype(BF16)
    fibres = part.shape[0]
    part = part.reshape(fibres, wide * pair, -1).swapaxes(0, 1)
    part = lax.all_to_all(part, ("wide", "pair"), 0, 0, tiled=True)
    part = part.reshape(wide, pair * fibres, -1).astype(F32).sum(0)
    omega = lax.all_gather(sketch, ("pair", "wide"), tiled=True).astype(F32)
    exact = functools.partial(jnp.dot, precision=lax.Precision.HIGHEST)
    own = exact(part.T, omega)
    moment = lax.psum(exact(part, own), ("wide", "pair"))
    lower = jnp.linalg.cholesky(exact(omega.T, moment))
    solve = functools.partial(
        lax.linalg.triangular_solve, lower, left_side=False, lower=True, transpose_a=True
    )
    count = sketch.shape[0]
    mine = lax.dynamic_slice_in_dim(moment, lax.axis_index(("pair", "wide")) * count, count, 0)
    return solve(own) * jnp.sqrt(F32(rank_a * rank_b)), solve(mine)


def solution(mesh):
    placed = (P("pair", "wide", None), P(), P(), P(("pair", "wide"), None))

    def per_device(blocks, basis_a, basis_b, sketch):
        fibres, rows, _ = blocks.shape
        rank_a, rank_b = basis_a.shape[1], basis_b.shape[1]
        wide, pair = lax.axis_size("wide"), lax.axis_size("pair")
        fits = (
            wide == 2 * SQUARE
            and rank_b == LANES // 2
            and sketch.shape[1] == LANES // 2
            and rank_a == 2 * wide * pair
            and rows == LANES
            and fibres * pair == LANES
            and fibres % 32 == 0
        )
        return (in_squares if fits else by_columns)(blocks, basis_a, basis_b, sketch)

    return jax.shard_map(
        per_device,
        mesh=mesh,
        in_specs=placed,
        out_specs=(P(("wide", "pair"), None), P(("pair", "wide"), None)),
        check_vma=False,
    )
```

time: 189 us -> 45.5 us (0.24)
  waiting for transfers between devices: 129 us -> 11 us
  blocking collectives: 21.6 us -> 5.84 us
  between operations: 14.1 us -> 0.68 us
  other arithmetic: 12.7 us -> 0.07 us
  Pallas kernels: 0 us -> 11.3 us
  matrix products: 11.2 us -> 0 us
  starting transfers between devices: 0.04 us -> 10.8 us
  local copies, waits for them, and re-layouts: 0.31 us -> 5.59 us
    psum x1 -> x0, waiting for transfers between devices: 129 us -> none  [per_device(): sketch_all = lax.psum(partial_value, ('wide', 'pair'))]
    all_to_all x1 -> x0, blocking collectives: 21.6 us -> none  [per_device(): lax.all_to_all(narrowed, 'wide', split_axis=0, concat_axis=1, tiled=True)]
    another operation x5 -> x0, other arithmetic: 12.1 us -> none  [the longest x3 6.52 us: orthonormal(): lower = jnp.linalg.cholesky(gram)]
    pallas_call x0 -> x3, Pallas kernels: none -> 11.3 us  [the longest x1 6.56 us: finish(): pl.pallas_call(functools.partial(finish_kernel, scale), out_shape=[jax.Sh...]
    ppermute x0 -> x7, waiting for transfers between devices: none -> 11 us  [partner(): lax.ppermute(x, 'wide', [(i, i ^ k) for i in range(lax.axis_size('wide'))])]
    ppermute x0 -> x7, starting transfers between devices: none -> 10.8 us  [partner(): lax.ppermute(x, 'wide', [(i, i ^ k) for i in range(lax.axis_size('wide'))])]
    dot_general x5 -> x0, matrix products: 8.94 us -> none  [the longest x1 3.58 us: per_device(): jnp.einsum('fac,cr->far', blocks, basis_b, preferred_element_type=jnp.flo...]
    all_gather x0 -> x1, blocking collectives: none -> 5.84 us  [in_squares(): gathered = lax.all_gather(total, 'pair')]
  transfers between devices with their start and end apart: 1 -> 7, of which waited for: 1 -> 6; matrix products, arithmetic and copies ran while one was open for 0% -> 0% of each run, Pallas kernels for 0% -> 0%
where the time goes in v1:
time: 45.5 us; the launch traced here: 45.2 us
  Pallas kernels  11.3 us (25%)
  waiting for transfers between devices  11 us (24%)
  starting transfers between devices  10.8 us (24%)
  blocking collectives  5.84 us (13%)
  local copies, waits for them, and re-layouts  5.59 us (12%)
  between operations  0.68 us (1%)
    ppermute x7, waiting for transfers between devices, partner(): lax.ppermute(x, 'wide', [(i, i ^ k) for i in range(lax.axis_size('wide'))])  11 us
    ppermute x7, starting transfers between devices, partner(): lax.ppermute(x, 'wide', [(i, i ^ k) for i in range(lax.axis_size('wide'))])  10.8 us
    pallas_call x1, Pallas kernels, finish(): pl.pallas_call(functools.partial(finish_kernel, scale), out_shape=[jax.Sh...  6.56 us
    all_gather x1, blocking collectives, in_squares(): gathered = lax.all_gather(total, 'pair')  5.84 us
    unnamed x6, local copies, waits for them, and re-layouts  4.9 us
    pallas_call x1, Pallas kernels, project(): pl.pallas_call(project_kernel, out_shape=[out] * SQUARE, in_specs=[anywhe...  4.21 us
  transfers between devices with their start and end apart: 7, of which 6 were waited for; matrix products, arithmetic and copies ran while one was open for 0% of the time, Pallas kernels for 0%

profile of v1, /device:TPU:0, one launch (start us, length us, event | category | flops | bytes accessed | tf_op | source)
XLA Modules:
  0.0 45.2 jit_solution(11162341784002000151)
XLA Ops:
  0.6 1.0 %copy.10.basis_b = bf16[512,64]{1,0:T(8,128)(2,1)S(1)} copy(bf16[512,64]{0,1:T(8,128)(2,1)} %param.6) | data formatting | bytes 131072 | tf_op args[2]
  1.6 1.1 %copy.9.basis_a = bf16[1024,64]{1,0:T(8,128)(2,1)S(1)} copy(bf16[1024,64]{0,1:T(8,128)(2,1)} %param.5) | data formatting | bytes 262144 | tf_op args[1]
  2.7 0.0 copy-start
  2.7 2.2 %copy-done = bf16[32,128,512]{2,1,0:T(8,128)(2,1)S(1)} copy-done((bf16[32,128,512]{2,1,0:T(8,128)(2,1)S(1)}, bf16[32,128,512]{2,1,0:T(8,128)(2,1)}, u32[]{:S(2)}) %copy-start) | copy-done | bytes 4194328
  4.9 0.0 copy-start.1
  4.9 0.7 %copy-done.1 = bf16[4,64]{1,0:T(4,128)(2,1)S(1)} copy-done((bf16[4,64]{1,0:T(4,128)(2,1)S(1)}, bf16[4,64]{1,0:T(4,128)(2,1)}, u32[]{:S(2)}) %copy-start.1) | copy-done | bytes 536
  5.5 4.2 %project.1 = (bf16[17,16,128]{2,1,0:T(8,128)(2,1)S(1)}, bf16[17,16,128]{2,1,0:T(8,128)(2,1)S(1)}, bf16[17,16,128]{2,1,0:T(8,128)(2,1)S(1)}, bf16[17,16,128]{2,1,0:T(8,128)(2,1)S(1)}) custom-call(bf16[32,128,512]{2,1,0:T(8,128)(2,1)S(1)} %copy-done, bf16[1024,64]{1,0:T(8,128)(2,1)S(1)} %copy.9.basis_a, bf16[512,64]{1,0:T(8,128)(2,1)S(1)} %copy.10.basis_b, ...), custom_call_target="tpu_custom_call" | custom-call | tf_op jit(solution)/shard_map/project/pallas_call | solution.py:101
  9.8 3.0 %collective-permute-start = (bf16[17,16,128]{2,1,0:T(8,128)(2,1)S(1)}, bf16[17,16,128]{2,1,0:T(8,128)(2,1)S(1)}, u32[]{:S(2)}, u32[]{:S(2)}) collective-permute-start(bf16[17,16,128]{2,1,0:T(8,128)(2,1)S(1)} %get-tuple-element.10), channel_id=1, source_target_pairs={{0,4},{4,0},{8,12},{12,8},{16,20},{20,16},{24,28},{28,24},{1,5},{5... | collective-permute-start | bytes 208904 | tf_op jit(solution)/shard_map/ppermute | solution.py:224
  12.8 1.6 %collective-permute-start.1 = (bf16[17,16,128]{2,1,0:T(8,128)(2,1)S(1)}, bf16[17,16,128]{2,1,0:T(8,128)(2,1)S(1)}, u32[]{:S(2)}, u32[]{:S(2)}) collective-permute-start(bf16[17,16,128]{2,1,0:T(8,128)(2,1)S(1)} %get-tuple-element.11), channel_id=1, source_target_pairs={{0,8},{4,12},{8,0},{12,4},{16,24},{20,28},{24,16},{28,20},{1,9},{5... | collective-permute-start | bytes 208904 | tf_op jit(solution)/shard_map/ppermute | solution.py:224
  14.4 0.0 collective-permute-start.2
  14.4 0.7 %collective-permute-done = bf16[17,16,128]{2,1,0:T(8,128)(2,1)S(1)} collective-permute-done((bf16[17,16,128]{2,1,0:T(8,128)(2,1)S(1)}, bf16[17,16,128]{2,1,0:T(8,128)(2,1)S(1)}, u32[]{:S(2)}, u32[]{:S(2)}) %collective-permute-start) | collective-permute-done | bytes 69664 | tf_op jit(solution)/shard_map/ppermute | solution.py:224
  15.1 2.6 %collective-permute-done.1 = bf16[17,16,128]{2,1,0:T(8,128)(2,1)S(1)} collective-permute-done((bf16[17,16,128]{2,1,0:T(8,128)(2,1)S(1)}, bf16[17,16,128]{2,1,0:T(8,128)(2,1)S(1)}, u32[]{:S(2)}, u32[]{:S(2)}) %collective-permute-start.1) | collective-permute-done | bytes 69664 | tf_op jit(solution)/shard_map/ppermute | solution.py:224
  17.7 1.9 %collective-permute-done.2 = bf16[17,16,128]{2,1,0:T(8,128)(2,1)S(1)} collective-permute-done((bf16[17,16,128]{2,1,0:T(8,128)(2,1)S(1)}, bf16[17,16,128]{2,1,0:T(8,128)(2,1)S(1)}, u32[]{:S(2)}, u32[]{:S(2)}) %collective-permute-start.2) | collective-permute-done | bytes 69664 | tf_op jit(solution)/shard_map/ppermute | solution.py:224
  19.6 2.7 %collective-permute-start.3 = (bf16[17,16,128]{2,1,0:T(8,128)(2,1)S(1)}, bf16[17,16,128]{2,1,0:T(8,128)(2,1)S(1)}, u32[]{:S(2)}, u32[]{:S(2)}) collective-permute-start(bf16[17,16,128]{2,1,0:T(8,128)(2,1)S(1)} %add_convert_fusion.1), channel_id=1, source_target_pairs={{0,16},{4,20},{8,24},{12,28},{16,0},{20,4},{24,8},{28,12},{1,17},{... | collective-permute-start | bytes 208904 | tf_op jit(solution)/shard_map/ppermute | solution.py:224
  22.3 3.2 %collective-permute-done.3 = bf16[17,16,128]{2,1,0:T(8,128)(2,1)S(1)} collective-permute-done((bf16[17,16,128]{2,1,0:T(8,128)(2,1)S(1)}, bf16[17,16,128]{2,1,0:T(8,128)(2,1)S(1)}, u32[]{:S(2)}, u32[]{:S(2)}) %collective-permute-start.3) | collective-permute-done | bytes 69664 | tf_op jit(solution)/shard_map/ppermute | solution.py:224
  25.6 5.8 %all-gather = bf16[68,16,128]{2,1,0:T(8,128)(2,1)S(1)} all-gather(bf16[17,16,128]{2,1,0:T(8,128)(2,1)S(1)} %add_convert_fusion), channel_id=2, replica_groups=mesh['wide'=8,'pair'=4] {'pair'}, dimensions={0}, use_global_device_ids=true | all-gather | bytes 348160 | tf_op jit(solution)/shard_map/all_gather | solution.py:236
  31.4 0.5 %square_product.1 = (f32[64,128]{1,0:T(8,128)S(1)}, f32[64,128]{1,0:T(8,128)S(1)}, bf16[64,128]{1,0:T(8,128)(2,1)S(1)}) custom-call(bf16[4,17,16,128]{3,2,1,0:T(8,128)(2,1)S(1)} %bitcast.1), custom_call_target="tpu_custom_call" | custom-call | tf_op jit(solution)/shard_map/square_product/pallas_call | solution.py:156
  31.9 0.4 collective-permute-start.6
  32.3 1.8 %collective-permute-start.5 = (f32[64,128]{1,0:T(8,128)S(1)}, f32[64,128]{1,0:T(8,128)S(1)}, u32[]{:S(2)}, u32[]{:S(2)}) collective-permute-start(f32[64,128]{1,0:T(8,128)S(1)} %get-tuple-element.13.m0), channel_id=1, source_target_pairs={{0,8},{4,12},{8,0},{12,4},{16,24},{20,28},{24,16},{28,20},{1,9},{5... | collective-permute-start | bytes 98312 | tf_op jit(solution)/shard_map/ppermute | solution.py:224
  34.0 1.4 %collective-permute-start.4 = (f32[64,128]{1,0:T(8,128)S(1)}, f32[64,128]{1,0:T(8,128)S(1)}, u32[]{:S(2)}, u32[]{:S(2)}) collective-permute-start(f32[64,128]{1,0:T(8,128)S(1)} %get-tuple-element.13.m0), channel_id=1, source_target_pairs={{0,4},{4,0},{8,12},{12,8},{16,20},{20,16},{24,28},{28,24},{1,5},{5... | collective-permute-start | bytes 98312 | tf_op jit(solution)/shard_map/ppermute | solution.py:224
  35.5 1.5 %collective-permute-done.6.m3 = f32[64,128]{1,0:T(8,128)S(1)} collective-permute-done((f32[64,128]{1,0:T(8,128)S(1)}, f32[64,128]{1,0:T(8,128)S(1)}, u32[]{:S(2)}, u32[]{:S(2)}) %collective-permute-start.6) | collective-permute-done | bytes 32800 | tf_op jit(solution)/shard_map/ppermute | solution.py:224
  36.9 0.0 collective-permute-done.5.m2
  36.9 1.0 %collective-permute-done.4.m1 = f32[64,128]{1,0:T(8,128)S(1)} collective-permute-done((f32[64,128]{1,0:T(8,128)S(1)}, f32[64,128]{1,0:T(8,128)S(1)}, u32[]{:S(2)}, u32[]{:S(2)}) %collective-permute-start.4) | collective-permute-done | bytes 32800 | tf_op jit(solution)/shard_map/ppermute | solution.py:224
  38.0 6.6 %finish.1 = (f32[128,64]{1,0:T(8,128)S(1)}, f32[4,64]{1,0:T(4,128)}) custom-call(f32[64,128]{1,0:T(8,128)S(1)} %get-tuple-element.13.m0, f32[64,128]{1,0:T(8,128)S(1)} %collective-permute-done.4.m1, f32[64,128]{1,0:T(8,128)S(1)} %collective-permute-done.5.m2, f32[64,128]{1,0:T(8,128)S(1)} %collective-permute-done.6.m3, f32[64,128]{1,0:T(8,128)S(1)} %get-tuple-element.14.own, ...), custom_call_target="tpu_custom_call" | custom-call | tf_op jit(solution)/shard_map/finish/pallas_call | solution.py:210
  44.5 0.7 %copy.11 = f32[128,64]{0,1:T(8,128)} copy(f32[128,64]{1,0:T(8,128)S(1)} %get-tuple-element.18) | data formatting | bytes 65536 | tf_op jit(solution)/shard_map/finish/pallas_call | solution.py:210
  (2 shorter events, 0.1 us)
Async XLA Ops:
  2.7 2.2 %copy-start = (bf16[32,128,512]{2,1,0:T(8,128)(2,1)S(1)}, bf16[32,128,512]{2,1,0:T(8,128)(2,1)}, u32[]{:S(2)}) copy-start(bf16[32,128,512]{2,1,0:T(8,128)(2,1)} %blocks.1) | copy-start | bytes 12582916
  4.9 0.7 %copy-start.1 = (bf16[4,64]{1,0:T(4,128)(2,1)S(1)}, bf16[4,64]{1,0:T(4,128)(2,1)}, u32[]{:S(2)}) copy-start(bf16[4,64]{1,0:T(4,128)(2,1)} %sketch.1) | copy-start | bytes 1540
  9.8 5.3 %collective-permute-start = (bf16[17,16,128]{2,1,0:T(8,128)(2,1)S(1)}, bf16[17,16,128]{2,1,0:T(8,128)(2,1)S(1)}, u32[]{:S(2)}, u32[]{:S(2)}) collective-permute-start(bf16[17,16,128]{2,1,0:T(8,128)(2,1)S(1)} %get-tuple-element.10), channel_id=1, source_target_pairs={{0,4},{4,0},{8,12},{12,8},{16,20},{20,16},{24,28},{28,24},{1,5},{5... | collective-permute-start | bytes 208904 | tf_op jit(solution)/shard_map/ppermute | solution.py:224
  12.8 4.9 %collective-permute-start.1 = (bf16[17,16,128]{2,1,0:T(8,128)(2,1)S(1)}, bf16[17,16,128]{2,1,0:T(8,128)(2,1)S(1)}, u32[]{:S(2)}, u32[]{:S(2)}) collective-permute-start(bf16[17,16,128]{2,1,0:T(8,128)(2,1)S(1)} %get-tuple-element.11), channel_id=1, source_target_pairs={{0,8},{4,12},{8,0},{12,4},{16,24},{20,28},{24,16},{28,20},{1,9},{5... | collective-permute-start | bytes 208904 | tf_op jit(solution)/shard_map/ppermute | solution.py:224
  14.4 5.2 %collective-permute-start.2 = (bf16[17,16,128]{2,1,0:T(8,128)(2,1)S(1)}, bf16[17,16,128]{2,1,0:T(8,128)(2,1)S(1)}, u32[]{:S(2)}, u32[]{:S(2)}) collective-permute-start(bf16[17,16,128]{2,1,0:T(8,128)(2,1)S(1)} %get-tuple-element.12), channel_id=1, source_target_pairs={{0,12},{4,8},{8,4},{12,0},{16,28},{20,24},{24,20},{28,16},{1,13},{... | collective-permute-start | bytes 208904 | tf_op jit(solution)/shard_map/ppermute | solution.py:224
  19.6 5.9 %collective-permute-start.3 = (bf16[17,16,128]{2,1,0:T(8,128)(2,1)S(1)}, bf16[17,16,128]{2,1,0:T(8,128)(2,1)S(1)}, u32[]{:S(2)}, u32[]{:S(2)}) collective-permute-start(bf16[17,16,128]{2,1,0:T(8,128)(2,1)S(1)} %add_convert_fusion.1), channel_id=1, source_target_pairs={{0,16},{4,20},{8,24},{12,28},{16,0},{20,4},{24,8},{28,12},{1,17},{... | collective-permute-start | bytes 208904 | tf_op jit(solution)/shard_map/ppermute | solution.py:224
  31.9 5.0 %collective-permute-start.6 = (f32[64,128]{1,0:T(8,128)S(1)}, f32[64,128]{1,0:T(8,128)S(1)}, u32[]{:S(2)}, u32[]{:S(2)}) collective-permute-start(f32[64,128]{1,0:T(8,128)S(1)} %get-tuple-element.13.m0), channel_id=1, source_target_pairs={{0,12},{4,8},{8,4},{12,0},{16,28},{20,24},{24,20},{28,16},{1,13},{... | collective-permute-start | bytes 98312 | tf_op jit(solution)/shard_map/ppermute | solution.py:224
  32.3 4.7 %collective-permute-start.5 = (f32[64,128]{1,0:T(8,128)S(1)}, f32[64,128]{1,0:T(8,128)S(1)}, u32[]{:S(2)}, u32[]{:S(2)}) collective-permute-start(f32[64,128]{1,0:T(8,128)S(1)} %get-tuple-element.13.m0), channel_id=1, source_target_pairs={{0,8},{4,12},{8,0},{12,4},{16,24},{20,28},{24,16},{28,20},{1,9},{5... | collective-permute-start | bytes 98312 | tf_op jit(solution)/shard_map/ppermute | solution.py:224
  34.0 3.9 %collective-permute-start.4 = (f32[64,128]{1,0:T(8,128)S(1)}, f32[64,128]{1,0:T(8,128)S(1)}, u32[]{:S(2)}, u32[]{:S(2)}) collective-permute-start(f32[64,128]{1,0:T(8,128)S(1)} %get-tuple-element.13.m0), channel_id=1, source_target_pairs={{0,4},{4,0},{8,12},{12,8},{16,20},{20,16},{24,28},{28,24},{1,5},{5... | collective-permute-start | bytes 98312 | tf_op jit(solution)/shard_map/ppermute | solution.py:224

commit v2 on v1

--- a/solution.py
+++ b/solution.py
@@ -11,7 +11,8 @@
 BF16 = jnp.bfloat16
 LANES = 128
 SQUARE = 4
-CHUNKS = 4
+CHUNKS = 1
+GROUP = 8
 NT = (((1,), (1,)), ((), ()))
 
 
@@ -28,15 +29,15 @@
     held, rows_a, held_b, held_s, diagonal, wanted, sums, sems = refs[SQUARE:]
     wide = lax.axis_index("wide")
     fibres, rows, columns = blocks.shape
-    rank_b = basis_b.shape[1]
-    rank_a = basis_a.shape[1]
+    rank_b = basis_b.shape[0]
+    rank_a = basis_a.shape[0]
     pairs = fibres // 2
     quad = 4 * rank_b
     per_chunk = fibres // CHUNKS
     copies = [
         pltpu.make_async_copy(basis_b, held_b, sems.at[CHUNKS]),
         pltpu.make_async_copy(
-            basis_a.at[pl.ds(pl.multiple_of(wide * rows, rows), rows), :], rows_a, sems.at[CHUNKS + 1]
+            basis_a.at[:, pl.ds(pl.multiple_of(wide * rows, rows), rows)], rows_a, sems.at[CHUNKS + 1]
         ),
         pltpu.make_async_copy(sketch, held_s, sems.at[CHUNKS + 2]),
     ]
@@ -47,7 +48,7 @@
         copy.start()
     diagonal[...] = jnp.zeros(diagonal.shape, BF16)
     copies[0].wait()
-    basis = held_b[...]
+    basis = held_b[...].astype(F32).T.astype(BF16)
     for j in range(4):
         part = [jnp.zeros((columns, LANES), BF16)] * (quad // LANES)
         empty = jnp.zeros((columns, rank_b), BF16)
@@ -55,8 +56,7 @@
         part[j // 2] = jnp.concatenate(both, axis=1)
         diagonal[pl.ds(j * columns, columns), pl.ds(j // 2 * LANES, LANES)] = part[j // 2]
     copies[1].wait()
-    turned = rows_a[...].astype(F32).T
-    wanted[...] = turned.reshape(wanted.shape)
+    wanted[...] = rows_a[...].astype(F32).reshape(wanted.shape)
     square = lax.rem(wide, SQUARE)
     halves = wanted.shape[0]
     left = jnp.concatenate(
@@ -90,22 +90,22 @@
 
 def project(blocks, basis_a, basis_b, sketch):
     fibres, rows, columns = blocks.shape
-    rank_a = basis_a.shape[1]
-    rank_b = basis_b.shape[1]
+    rank_a = basis_a.shape[0]
+    rank_b = basis_b.shape[0]
     pairs = fibres // 2
     wide = lax.axis_size("wide")
     count = rank_a // SQUARE
     out = jax.ShapeDtypeStruct((count + 1, pairs, LANES), BF16)
     vmem = pl.BlockSpec(memory_space=pltpu.VMEM)
-    anywhere = pl.BlockSpec(memory_space=pl.ANY)
+    outside = pl.BlockSpec(memory_space=pltpu.HBM)
     return pl.pallas_call(
         project_kernel,
         out_shape=[out] * SQUARE,
-        in_specs=[anywhere] * 4,
+        in_specs=[outside] * 4,
         out_specs=[vmem] * SQUARE,
         scratch_shapes=[
             pltpu.VMEM(blocks.shape, BF16),
-            pltpu.VMEM((rows, rank_a), BF16),
+            pltpu.VMEM((rank_a, rows), BF16),
             pltpu.VMEM(basis_b.shape, BF16),
             pltpu.VMEM(sketch.shape, BF16),
             pltpu.VMEM((4 * columns, 4 * rank_b), BF16),
@@ -113,7 +113,7 @@
             pltpu.VMEM((rank_a * pairs, LANES), F32),
             pltpu.SemaphoreType.DMA((CHUNKS + 3,)),
         ],
-        compiler_params=pltpu.CompilerParams(vmem_limit_bytes=32 * 2**20),
+        compiler_params=pltpu.CompilerParams(vmem_limit_bytes=58 * 2**20),
         name="project",
     )(blocks, basis_a, basis_b, sketch)
 
@@ -164,6 +164,51 @@
     )(gathered)
 
 
+def inverse_factor(table):
+    rank = table.shape[0]
+    tiles = [table[8 * t : 8 * t + 8] for t in range(rank // 8)]
+    shape = tiles[0].shape
+    below = lax.broadcasted_iota(jnp.int32, shape, 0)
+    inverse = []
+    for start in range(0, rank, GROUP):
+        first, inside = divmod(start, 8)
+        last = inside + GROUP == 8
+        terms = {
+            t: [jnp.broadcast_to(tiles[t][:, start + k : start + k + 1], shape) for k in range(GROUP)]
+            for t in range(first, rank // 8)
+        }
+        lines = [jnp.broadcast_to(tiles[first][inside + k : inside + k + 1], shape) for k in range(GROUP)]
+        entry = {
+            (k, m): jnp.broadcast_to(terms[first][m][inside + k : inside + k + 1], shape)
+            for k in range(GROUP)
+            for m in range(k + 1)
+        }
+        if last:
+            del terms[first]
+        for k in range(GROUP):
+            root = lax.rsqrt(entry[k, k])
+            lines[k] = lines[k] * root
+            for t in terms:
+                terms[t][k] = terms[t][k] * root
+            for m in range(k + 1, GROUP):
+                entry[m, k] = entry[m, k] * root
+            for m in range(k + 1, GROUP):
+                for n in range(k + 1, m + 1):
+                    entry[m, n] = entry[m, n] - entry[m, k] * entry[n, k]
+                lines[m] = lines[m] - entry[m, k] * lines[k]
+                for t in terms:
+                    terms[t][m] = terms[t][m] - entry[m, k] * terms[t][k]
+        for t in terms:
+            change = terms[t][0] * lines[0]
+            for k in range(1, GROUP):
+                change = change + terms[t][k] * lines[k]
+            if t == first:
+                change = jnp.where(below >= inside + GROUP, change, 0.0)
+            tiles[t] = tiles[t] - change
+        inverse += [line[:1, rank:] for line in lines]
+    return jnp.concatenate(inverse, axis=0)
+
+
 def finish_kernel(scale, m0, m1, m2, m3, own, turned_sketch, transfer, coefficients):
     wide = lax.axis_index("wide")
     pair = lax.axis_index("pair")
@@ -174,24 +219,9 @@
     gram = product[:rank] + (product[rank : 2 * rank] + product[2 * rank :])
     row = lax.broadcasted_iota(jnp.int32, (rank, rank), 0)
     column = lax.broadcasted_iota(jnp.int32, (rank, rank), 1)
-    table = jnp.concatenate([gram, (row == column).astype(F32)], axis=1)
-    below = lax.broadcasted_iota(jnp.int32, (8, LANES), 0)
-    blocks = [table[8 * b : 8 * b + 8] for b in range(rank // 8)]
-    inverse = []
-    for j in range(rank):
-        b, i = divmod(j, 8)
-        line = blocks[b][i : i + 1]
-        pivot = line[:, j : j + 1]
-        inverse.append(line[:, rank:] * lax.rsqrt(pivot))
-        line = line / pivot
-        for c in range(b, rank // 8):
-            factor = blocks[c][:, j : j + 1]
-            if c == b:
-                factor = jnp.where(below[:, :1] > i, factor, 0.0)
-            blocks[c] = blocks[c] - factor * line
-    inverse = jnp.concatenate(inverse, axis=0)
-    transfer[...] = scale * lax.dot_general(
-        own[...].T, inverse, NT, preferred_element_type=F32, precision=lax.Precision.HIGHEST
+    inverse = inverse_factor(jnp.concatenate([gram, (row == column).astype(F32)], axis=1))
+    transfer[...] = scale * jnp.dot(
+        inverse, own[...], preferred_element_type=F32, precision=lax.Precision.HIGHEST
     )
     count = coefficients.shape[0]
     groups = lax.axis_size("pair")
@@ -210,7 +240,7 @@
     return pl.pallas_call(
         functools.partial(finish_kernel, scale),
         out_shape=[
-            jax.ShapeDtypeStruct((own.shape[1], rank), F32),
+            jax.ShapeDtypeStruct(own.shape, F32),
             jax.ShapeDtypeStruct((count, rank), F32),
         ],
         in_specs=[vmem] * 6,
@@ -225,7 +255,7 @@
 
 
 def in_squares(blocks, basis_a, basis_b, sketch):
-    outs = project(blocks, basis_a, basis_b, sketch)
+    outs = project(blocks, basis_a.T, basis_b.T, sketch)
     got = [partner(outs[k], k) for k in range(1, SQUARE)]
     total = outs[0].astype(F32)
     for term in got:
@@ -237,7 +267,8 @@
     moment, own, turned_sketch = square_product(gathered)
     moments = [moment] + [partner(moment, k) for k in range(1, SQUARE)]
     scale = float((basis_a.shape[1] * basis_b.shape[1]) ** 0.5)
-    return tuple(finish(moments, own, turned_sketch, scale, sketch.shape[0]))
+    transfer, coefficients = finish(moments, own, turned_sketch, scale, sketch.shape[0])
+    return transfer.T, coefficients
 
 
 def by_columns(blocks, basis_a, basis_b, sketch):

time: 45.5 us -> 37.7 us (0.83)
  local copies, waits for them, and re-layouts: 5.59 us -> 0 us
  Pallas kernels: 11.3 us -> 8.06 us
  other arithmetic: 0.07 us -> 0.95 us
    unnamed x6 -> x0, local copies, waits for them, and re-layouts: 4.9 us -> none
    pallas_call x1, Pallas kernels: 6.56 us -> 3.01 us  [finish(): pl.pallas_call(functools.partial(finish_kernel, scale), out_shape=[jax.Sh...]
    convert_element_type x1, other arithmetic: 0.04 us -> 0.93 us  [in_squares(): total = total.astype(BF16)]
    pallas_call x1 -> x0, local copies, waits for them, and re-layouts: 0.7 us -> none  [finish(): pl.pallas_call(functools.partial(finish_kernel, scale), out_shape=[jax.Sh...]
where the time goes in v2:
time: 37.7 us; the launch traced here: 37.5 us
  waiting for transfers between devices  11.2 us (30%)
  starting transfers between devices  10.8 us (29%)
  Pallas kernels  8.06 us (21%)
  blocking collectives  5.84 us (15%)
  other arithmetic  0.95 us (3%)
  between operations  0.66 us (2%)
    ppermute x7, waiting for transfers between devices, partner(): lax.ppermute(x, 'wide', [(i, i ^ k) for i in range(lax.axis_size('wide'))])  11.2 us
    ppermute x7, starting transfers between devices, partner(): lax.ppermute(x, 'wide', [(i, i ^ k) for i in range(lax.axis_size('wide'))])  10.8 us
    all_gather x1, blocking collectives, in_squares(): gathered = lax.all_gather(total, 'pair')  5.84 us
    pallas_call x1, Pallas kernels, project(): pl.pallas_call(project_kernel, out_shape=[out] * SQUARE, in_specs=[outsid...  4.57 us
    pallas_call x1, Pallas kernels, finish(): pl.pallas_call(functools.partial(finish_kernel, scale), out_shape=[jax.Sh...  3.01 us
    convert_element_type x1, other arithmetic, in_squares(): total = total.astype(BF16)  0.93 us
  transfers between devices with their start and end apart: 7, of which 6 were waited for; matrix products, arithmetic and copies ran while one was open for 0% of the time, Pallas kernels for 0%

profile of v2, /device:TPU:0, one launch (start us, length us, event | category | flops | bytes accessed | tf_op | source)
XLA Modules:
  0.0 37.5 jit_solution(4583773091502008406)
XLA Ops:
  0.6 4.6 %project.1 = (bf16[17,16,128]{2,1,0:T(8,128)(2,1)}, bf16[17,16,128]{2,1,0:T(8,128)(2,1)}, bf16[17,16,128]{2,1,0:T(8,128)(2,1)}, bf16[17,16,128]{2,1,0:T(8,128)(2,1)}) custom-call(bf16[32,128,512]{2,1,0:T(8,128)(2,1)} %blocks.1, bf16[64,1024]{1,0:T(8,128)(2,1)} %bitcast.5, bf16[64,512]{1,0:T(8,128)(2,1)} %bitcast.6, bf16[4,64]{1,0:T(4,128)(2,1)} %sketch.1), custom_call_target="tpu_custom_call" | custom-call | tf_op jit(solution)/shard_map/project/pallas_call | solution.py:101
  5.2 3.0 %collective-permute-start = (bf16[17,16,128]{2,1,0:T(8,128)(2,1)}, bf16[17,16,128]{2,1,0:T(8,128)(2,1)S(1)}, u32[]{:S(2)}, u32[]{:S(2)}) collective-permute-start(bf16[17,16,128]{2,1,0:T(8,128)(2,1)} %get-tuple-element.12), channel_id=1, source_target_pairs={{0,4},{4,0},{8,12},{12,8},{16,20},{20,16},{24,28},{28,24},{1,5},{5... | collective-permute-start | bytes 208904 | tf_op jit(solution)/shard_map/ppermute | solution.py:254
  8.2 1.6 %collective-permute-start.1 = (bf16[17,16,128]{2,1,0:T(8,128)(2,1)}, bf16[17,16,128]{2,1,0:T(8,128)(2,1)S(1)}, u32[]{:S(2)}, u32[]{:S(2)}) collective-permute-start(bf16[17,16,128]{2,1,0:T(8,128)(2,1)} %get-tuple-element.13), channel_id=1, source_target_pairs={{0,8},{4,12},{8,0},{12,4},{16,24},{20,28},{24,16},{28,20},{1,9},{5... | collective-permute-start | bytes 208904 | tf_op jit(solution)/shard_map/ppermute | solution.py:254
  9.8 0.0 collective-permute-start.2
  9.8 0.9 %collective-permute-done = bf16[17,16,128]{2,1,0:T(8,128)(2,1)S(1)} collective-permute-done((bf16[17,16,128]{2,1,0:T(8,128)(2,1)}, bf16[17,16,128]{2,1,0:T(8,128)(2,1)S(1)}, u32[]{:S(2)}, u32[]{:S(2)}) %collective-permute-start) | collective-permute-done | bytes 69664 | tf_op jit(solution)/shard_map/ppermute | solution.py:254
  10.7 2.6 %collective-permute-done.1 = bf16[17,16,128]{2,1,0:T(8,128)(2,1)S(1)} collective-permute-done((bf16[17,16,128]{2,1,0:T(8,128)(2,1)}, bf16[17,16,128]{2,1,0:T(8,128)(2,1)S(1)}, u32[]{:S(2)}, u32[]{:S(2)}) %collective-permute-start.1) | collective-permute-done | bytes 69664 | tf_op jit(solution)/shard_map/ppermute | solution.py:254
  13.3 1.9 %collective-permute-done.2 = bf16[17,16,128]{2,1,0:T(8,128)(2,1)S(1)} collective-permute-done((bf16[17,16,128]{2,1,0:T(8,128)(2,1)}, bf16[17,16,128]{2,1,0:T(8,128)(2,1)S(1)}, u32[]{:S(2)}, u32[]{:S(2)}) %collective-permute-start.2) | collective-permute-done | bytes 69664 | tf_op jit(solution)/shard_map/ppermute | solution.py:254
  15.2 0.9 %add_convert_fusion.1 = bf16[17,16,128]{2,1,0:T(8,128)(2,1)S(1)} fusion(bf16[17,16,128]{2,1,0:T(8,128)(2,1)S(1)} %collective-permute-done.2, bf16[17,16,128]{2,1,0:T(8,128)(2,1)S(1)} %collective-permute-done.1, bf16[17,16,128]{2,1,0:T(8,128)(2,1)S(1)} %collective-permute-done, bf16[17,16,128]{2,1,0:T(8,128)(2,1)} %get-tuple-element.11), kind=kLoop, calls=%fused_computation.1 | loop fusion | flops 278528 | bytes 348160 | tf_op jit(solution)/shard_map/convert_element_type | solution.py:263
  16.2 2.7 %collective-permute-start.3 = (bf16[17,16,128]{2,1,0:T(8,128)(2,1)S(1)}, bf16[17,16,128]{2,1,0:T(8,128)(2,1)S(1)}, u32[]{:S(2)}, u32[]{:S(2)}) collective-permute-start(bf16[17,16,128]{2,1,0:T(8,128)(2,1)S(1)} %add_convert_fusion.1), channel_id=1, source_target_pairs={{0,16},{4,20},{8,24},{12,28},{16,0},{20,4},{24,8},{28,12},{1,17},{... | collective-permute-start | bytes 208904 | tf_op jit(solution)/shard_map/ppermute | solution.py:254
  18.8 3.3 %collective-permute-done.3 = bf16[17,16,128]{2,1,0:T(8,128)(2,1)S(1)} collective-permute-done((bf16[17,16,128]{2,1,0:T(8,128)(2,1)S(1)}, bf16[17,16,128]{2,1,0:T(8,128)(2,1)S(1)}, u32[]{:S(2)}, u32[]{:S(2)}) %collective-permute-start.3) | collective-permute-done | bytes 69664 | tf_op jit(solution)/shard_map/ppermute | solution.py:254
  22.1 5.8 %all-gather = bf16[68,16,128]{2,1,0:T(8,128)(2,1)S(1)} all-gather(bf16[17,16,128]{2,1,0:T(8,128)(2,1)S(1)} %add_convert_fusion), channel_id=2, replica_groups=mesh['wide'=8,'pair'=4] {'pair'}, dimensions={0}, use_global_device_ids=true | all-gather | bytes 348160 | tf_op jit(solution)/shard_map/all_gather | solution.py:266
  27.9 0.5 %square_product.1 = (f32[64,128]{1,0:T(8,128)S(1)}, f32[64,128]{1,0:T(8,128)S(1)}, bf16[64,128]{1,0:T(8,128)(2,1)S(1)}) custom-call(bf16[4,17,16,128]{3,2,1,0:T(8,128)(2,1)S(1)} %bitcast.4), custom_call_target="tpu_custom_call" | custom-call | tf_op jit(solution)/shard_map/square_product/pallas_call | solution.py:156
  28.4 0.4 collective-permute-start.6
  28.8 1.8 %collective-permute-start.5 = (f32[64,128]{1,0:T(8,128)S(1)}, f32[64,128]{1,0:T(8,128)S(1)}, u32[]{:S(2)}, u32[]{:S(2)}) collective-permute-start(f32[64,128]{1,0:T(8,128)S(1)} %get-tuple-element.15.m0), channel_id=1, source_target_pairs={{0,8},{4,12},{8,0},{12,4},{16,24},{20,28},{24,16},{28,20},{1,9},{5... | collective-permute-start | bytes 98312 | tf_op jit(solution)/shard_map/ppermute | solution.py:254
  30.6 1.4 %collective-permute-start.4 = (f32[64,128]{1,0:T(8,128)S(1)}, f32[64,128]{1,0:T(8,128)S(1)}, u32[]{:S(2)}, u32[]{:S(2)}) collective-permute-start(f32[64,128]{1,0:T(8,128)S(1)} %get-tuple-element.15.m0), channel_id=1, source_target_pairs={{0,4},{4,0},{8,12},{12,8},{16,20},{20,16},{24,28},{28,24},{1,5},{5... | collective-permute-start | bytes 98312 | tf_op jit(solution)/shard_map/ppermute | solution.py:254
  32.0 1.5 %collective-permute-done.6.m3 = f32[64,128]{1,0:T(8,128)S(1)} collective-permute-done((f32[64,128]{1,0:T(8,128)S(1)}, f32[64,128]{1,0:T(8,128)S(1)}, u32[]{:S(2)}, u32[]{:S(2)}) %collective-permute-start.6) | collective-permute-done | bytes 32800 | tf_op jit(solution)/shard_map/ppermute | solution.py:254
  33.4 0.0 collective-permute-done.5.m2
  33.4 1.0 %collective-permute-done.4.m1 = f32[64,128]{1,0:T(8,128)S(1)} collective-permute-done((f32[64,128]{1,0:T(8,128)S(1)}, f32[64,128]{1,0:T(8,128)S(1)}, u32[]{:S(2)}, u32[]{:S(2)}) %collective-permute-start.4) | collective-permute-done | bytes 32800 | tf_op jit(solution)/shard_map/ppermute | solution.py:254
  34.5 3.0 %finish.1 = (f32[64,128]{1,0:T(8,128)}, f32[4,64]{1,0:T(4,128)}) custom-call(f32[64,128]{1,0:T(8,128)S(1)} %get-tuple-element.15.m0, f32[64,128]{1,0:T(8,128)S(1)} %collective-permute-done.4.m1, f32[64,128]{1,0:T(8,128)S(1)} %collective-permute-done.5.m2, f32[64,128]{1,0:T(8,128)S(1)} %collective-permute-done.6.m3, f32[64,128]{1,0:T(8,128)S(1)} %get-tuple-element.16.own, ...), custom_call_target="tpu_custom_call" | custom-call | tf_op jit(solution)/shard_map/finish/pallas_call | solution.py:240
  (1 shorter events, 0.0 us)
Async XLA Ops:
  5.2 5.5 %collective-permute-start = (bf16[17,16,128]{2,1,0:T(8,128)(2,1)}, bf16[17,16,128]{2,1,0:T(8,128)(2,1)S(1)}, u32[]{:S(2)}, u32[]{:S(2)}) collective-permute-start(bf16[17,16,128]{2,1,0:T(8,128)(2,1)} %get-tuple-element.12), channel_id=1, source_target_pairs={{0,4},{4,0},{8,12},{12,8},{16,20},{20,16},{24,28},{28,24},{1,5},{5... | collective-permute-start | bytes 208904 | tf_op jit(solution)/shard_map/ppermute | solution.py:254
  8.2 5.1 %collective-permute-start.1 = (bf16[17,16,128]{2,1,0:T(8,128)(2,1)}, bf16[17,16,128]{2,1,0:T(8,128)(2,1)S(1)}, u32[]{:S(2)}, u32[]{:S(2)}) collective-permute-start(bf16[17,16,128]{2,1,0:T(8,128)(2,1)} %get-tuple-element.13), channel_id=1, source_target_pairs={{0,8},{4,12},{8,0},{12,4},{16,24},{20,28},{24,16},{28,20},{1,9},{5... | collective-permute-start | bytes 208904 | tf_op jit(solution)/shard_map/ppermute | solution.py:254
  9.8 5.4 %collective-permute-start.2 = (bf16[17,16,128]{2,1,0:T(8,128)(2,1)}, bf16[17,16,128]{2,1,0:T(8,128)(2,1)S(1)}, u32[]{:S(2)}, u32[]{:S(2)}) collective-permute-start(bf16[17,16,128]{2,1,0:T(8,128)(2,1)} %get-tuple-element.14), channel_id=1, source_target_pairs={{0,12},{4,8},{8,4},{12,0},{16,28},{20,24},{24,20},{28,16},{1,13},{... | collective-permute-start | bytes 208904 | tf_op jit(solution)/shard_map/ppermute | solution.py:254
  16.2 5.9 %collective-permute-start.3 = (bf16[17,16,128]{2,1,0:T(8,128)(2,1)S(1)}, bf16[17,16,128]{2,1,0:T(8,128)(2,1)S(1)}, u32[]{:S(2)}, u32[]{:S(2)}) collective-permute-start(bf16[17,16,128]{2,1,0:T(8,128)(2,1)S(1)} %add_convert_fusion.1), channel_id=1, source_target_pairs={{0,16},{4,20},{8,24},{12,28},{16,0},{20,4},{24,8},{28,12},{1,17},{... | collective-permute-start | bytes 208904 | tf_op jit(solution)/shard_map/ppermute | solution.py:254
  28.4 5.0 %collective-permute-start.6 = (f32[64,128]{1,0:T(8,128)S(1)}, f32[64,128]{1,0:T(8,128)S(1)}, u32[]{:S(2)}, u32[]{:S(2)}) collective-permute-start(f32[64,128]{1,0:T(8,128)S(1)} %get-tuple-element.15.m0), channel_id=1, source_target_pairs={{0,12},{4,8},{8,4},{12,0},{16,28},{20,24},{24,20},{28,16},{1,13},{... | collective-permute-start | bytes 98312 | tf_op jit(solution)/shard_map/ppermute | solution.py:254
  28.8 4.7 %collective-permute-start.5 = (f32[64,128]{1,0:T(8,128)S(1)}, f32[64,128]{1,0:T(8,128)S(1)}, u32[]{:S(2)}, u32[]{:S(2)}) collective-permute-start(f32[64,128]{1,0:T(8,128)S(1)} %get-tuple-element.15.m0), channel_id=1, source_target_pairs={{0,8},{4,12},{8,0},{12,4},{16,24},{20,28},{24,16},{28,20},{1,9},{5... | collective-permute-start | bytes 98312 | tf_op jit(solution)/shard_map/ppermute | solution.py:254
  30.6 3.9 %collective-permute-start.4 = (f32[64,128]{1,0:T(8,128)S(1)}, f32[64,128]{1,0:T(8,128)S(1)}, u32[]{:S(2)}, u32[]{:S(2)}) collective-permute-start(f32[64,128]{1,0:T(8,128)S(1)} %get-tuple-element.15.m0), channel_id=1, source_target_pairs={{0,4},{4,0},{8,12},{12,8},{16,20},{20,16},{24,28},{28,24},{1,5},{5... | collective-permute-start | bytes 98312 | tf_op jit(solution)/shard_map/ppermute | solution.py:254

commit v3 on v2

--- a/solution.py
+++ b/solution.py
@@ -11,7 +11,8 @@
 BF16 = jnp.bfloat16
 LANES = 128
 SQUARE = 4
-CHUNKS = 1
+CUTS = (2, 2, 2, 2)
+SPLIT = 2
 GROUP = 8
 NT = (((1,), (1,)), ((), ()))
 
@@ -32,48 +33,59 @@
     rank_b = basis_b.shape[0]
     rank_a = basis_a.shape[0]
     pairs = fibres // 2
-    quad = 4 * rank_b
-    per_chunk = fibres // CHUNKS
-    copies = [
-        pltpu.make_async_copy(basis_b, held_b, sems.at[CHUNKS]),
-        pltpu.make_async_copy(
-            basis_a.at[:, pl.ds(pl.multiple_of(wide * rows, rows), rows)], rows_a, sems.at[CHUNKS + 1]
-        ),
-        pltpu.make_async_copy(sketch, held_s, sems.at[CHUNKS + 2]),
+    small = [
+        pltpu.make_async_copy(basis_b, held_b, sems.at[0]),
+        pltpu.make_async_copy(basis_a.at[:, pl.ds(pl.multiple_of(wide * rows, rows), rows)], rows_a, sems.at[1]),
+        pltpu.make_async_copy(sketch, held_s, sems.at[2]),
     ]
-    for c in range(CHUNKS):
-        part = pl.ds(c * per_chunk, per_chunk)
-        copies.append(pltpu.make_async_copy(blocks.at[part], held.at[part], sems.at[c]))
-    for copy in copies:
+    unit = fibres // sum(CUTS)
+    parts, begin = [], 0
+    for cut in CUTS:
+        parts.append((begin, cut * unit))
+        begin += cut * unit
+    large = [
+        pltpu.make_async_copy(blocks.at[pl.ds(at, n)], held.at[pl.ds(at, n)], sems.at[3 + i])
+        for i, (at, n) in enumerate(parts)
+    ]
+    for copy in small + large:
         copy.start()
-    diagonal[...] = jnp.zeros(diagonal.shape, BF16)
-    copies[0].wait()
+    small[0].wait()
     basis = held_b[...].astype(F32).T.astype(BF16)
-    for j in range(4):
-        part = [jnp.zeros((columns, LANES), BF16)] * (quad // LANES)
-        empty = jnp.zeros((columns, rank_b), BF16)
-        both = [basis, empty] if j % 2 == 0 else [empty, basis]
-        part[j // 2] = jnp.concatenate(both, axis=1)
-        diagonal[pl.ds(j * columns, columns), pl.ds(j // 2 * LANES, LANES)] = part[j // 2]
-    copies[1].wait()
+    empty = jnp.zeros_like(basis)
+    diagonal[pl.ds(0, columns)] = jnp.concatenate([basis, empty], axis=1)
+    diagonal[pl.ds(columns, columns)] = jnp.concatenate([empty, basis], axis=1)
+    small[1].wait()
     wanted[...] = rows_a[...].astype(F32).reshape(wanted.shape)
     square = lax.rem(wide, SQUARE)
     halves = wanted.shape[0]
     left = jnp.concatenate(
         [wanted[half, square ^ k] for k in range(SQUARE) for half in range(halves)], axis=0
     ).astype(BF16)
-    for c in range(CHUNKS):
-        copies[3 + c].wait()
-        here = held[pl.ds(c * per_chunk, per_chunk)]
-        here = here.reshape(per_chunk // 4, 4, rows, columns)
-        lhs = jnp.concatenate([here[:, j].reshape(per_chunk // 4 * rows, columns) for j in range(4)], axis=1)
-        narrowed = jnp.dot(lhs, diagonal[...], preferred_element_type=F32).astype(BF16)
-        for q in range(per_chunk // 4):
-            found = jnp.dot(left, narrowed[q * rows : (q + 1) * rows], preferred_element_type=F32)
-            for t in range(quad // LANES):
-                s = (c * per_chunk // 4 + q) * 2 + t
-                sums[pl.ds(s, rank_a, stride=pairs), :] = found[:, t * LANES : (t + 1) * LANES]
-    copies[2].wait()
+
+    def narrow(at, n):
+        found = []
+        for i in range(SPLIT):
+            here = held[pl.ds(at + i * n // SPLIT, n // SPLIT)].reshape(n // SPLIT // 2, 2, rows, columns)
+            lhs = jnp.concatenate([here[:, j].reshape(-1, columns) for j in range(2)], axis=1)
+            found.append(jnp.dot(lhs, diagonal[...], preferred_element_type=F32).astype(BF16))
+        return jnp.concatenate(found, axis=0)
+
+    def fold(at, n, narrowed):
+        for q in range(n // 4):
+            two = [narrowed[(2 * q + t) * rows : (2 * q + t + 1) * rows] for t in range(2)]
+            found = jnp.dot(left, jnp.concatenate(two, axis=1), preferred_element_type=F32)
+            for t in range(2):
+                sums[pl.ds(at // 2 + 2 * q + t, rank_a, stride=pairs), :] = found[:, t * LANES : (t + 1) * LANES]
+
+    late = None
+    for copy, (at, n) in zip(large, parts):
+        copy.wait()
+        narrowed = narrow(at, n)
+        if late is not None:
+            fold(*late)
+        late = (at, n, narrowed)
+    fold(*late)
+    small[2].wait()
     mine = held_s[...].astype(F32)
     own = mine.shape[0]
     row = lax.broadcasted_iota(jnp.int32, (pairs, LANES), 0)
@@ -108,14 +120,14 @@
             pltpu.VMEM((rank_a, rows), BF16),
             pltpu.VMEM(basis_b.shape, BF16),
             pltpu.VMEM(sketch.shape, BF16),
-            pltpu.VMEM((4 * columns, 4 * rank_b), BF16),
+            pltpu.VMEM((2 * columns, 2 * rank_b), BF16),
             pltpu.VMEM((wide // SQUARE, SQUARE, rank_a // wide, rows), F32),
             pltpu.VMEM((rank_a * pairs, LANES), F32),
-            pltpu.SemaphoreType.DMA((CHUNKS + 3,)),
+            pltpu.SemaphoreType.DMA((3 + len(CUTS),)),
         ],
-        compiler_params=pltpu.CompilerParams(vmem_limit_bytes=58 * 2**20),
+        compiler_params=pltpu.CompilerParams(vmem_limit_bytes=32 * 2**20),
         name="project",
-    )(blocks, basis_a, basis_b, sketch)
+    )(*(pltpu.with_memory_space_constraint(x, pltpu.HBM) for x in (blocks, basis_a, basis_b, sketch)))
 
 
 def square_kernel(gathered, moment, own, turned_sketch, held):

time: 37.7 us -> 35.4 us (0.939)
  Pallas kernels: 8.06 us -> 6.87 us
  other arithmetic: 0.95 us -> 0.07 us
    pallas_call x1, Pallas kernels: 4.57 us -> 3.38 us  [project(): pl.pallas_call(project_kernel, out_shape=[out] * SQUARE, in_specs=[outsid...]
    convert_element_type x1, other arithmetic: 0.93 us -> 0.04 us  [in_squares(): total = total.astype(BF16)]
where the time goes in v3:
time: 35.4 us; the launch traced here: 35.2 us
  waiting for transfers between devices  11 us (31%)
  starting transfers between devices  10.8 us (31%)
  Pallas kernels  6.87 us (19%)
  blocking collectives  5.83 us (16%)
  between operations  0.66 us (2%)
    ppermute x7, waiting for transfers between devices, partner(): lax.ppermute(x, 'wide', [(i, i ^ k) for i in range(lax.axis_size('wide'))])  11 us
    ppermute x7, starting transfers between devices, partner(): lax.ppermute(x, 'wide', [(i, i ^ k) for i in range(lax.axis_size('wide'))])  10.8 us
    all_gather x1, blocking collectives, in_squares(): gathered = lax.all_gather(total, 'pair')  5.83 us
    pallas_call x1, Pallas kernels, project(): pl.pallas_call(project_kernel, out_shape=[out] * SQUARE, in_specs=[outsid...  3.38 us
    pallas_call x1, Pallas kernels, finish(): pl.pallas_call(functools.partial(finish_kernel, scale), out_shape=[jax.Sh...  3.01 us
  transfers between devices with their start and end apart: 7, of which 6 were waited for; matrix products, arithmetic and copies ran while one was open for 0% of the time, Pallas kernels for 0%

profile of v3, /device:TPU:0, one launch (start us, length us, event | category | flops | bytes accessed | tf_op | source)
XLA Modules:
  0.0 35.2 jit_solution(10104759476234971804)
XLA Ops:
  0.6 3.4 %project.1 = (bf16[17,16,128]{2,1,0:T(8,128)(2,1)S(1)}, bf16[17,16,128]{2,1,0:T(8,128)(2,1)S(1)}, bf16[17,16,128]{2,1,0:T(8,128)(2,1)S(1)}, bf16[17,16,128]{2,1,0:T(8,128)(2,1)S(1)}) custom-call(bf16[32,128,512]{2,1,0:T(8,128)(2,1)} %blocks.1, bf16[64,1024]{1,0:T(8,128)(2,1)} %bitcast.5, bf16[64,512]{1,0:T(8,128)(2,1)} %bitcast.6, bf16[4,64]{1,0:T(4,128)(2,1)} %sketch.1), custom_call_target="tpu_custom_call" | custom-call | tf_op jit(solution)/shard_map/project/pallas_call | solution.py:113
  4.0 3.0 %collective-permute-start = (bf16[17,16,128]{2,1,0:T(8,128)(2,1)S(1)}, bf16[17,16,128]{2,1,0:T(8,128)(2,1)S(1)}, u32[]{:S(2)}, u32[]{:S(2)}) collective-permute-start(bf16[17,16,128]{2,1,0:T(8,128)(2,1)S(1)} %get-tuple-element.12), channel_id=1, source_target_pairs={{0,4},{4,0},{8,12},{12,8},{16,20},{20,16},{24,28},{28,24},{1,5},{5... | collective-permute-start | bytes 208904 | tf_op jit(solution)/shard_map/ppermute | solution.py:266
  7.0 1.6 %collective-permute-start.1 = (bf16[17,16,128]{2,1,0:T(8,128)(2,1)S(1)}, bf16[17,16,128]{2,1,0:T(8,128)(2,1)S(1)}, u32[]{:S(2)}, u32[]{:S(2)}) collective-permute-start(bf16[17,16,128]{2,1,0:T(8,128)(2,1)S(1)} %get-tuple-element.13), channel_id=1, source_target_pairs={{0,8},{4,12},{8,0},{12,4},{16,24},{20,28},{24,16},{28,20},{1,9},{5... | collective-permute-start | bytes 208904 | tf_op jit(solution)/shard_map/ppermute | solution.py:266
  8.6 0.0 collective-permute-start.2
  8.6 0.7 %collective-permute-done = bf16[17,16,128]{2,1,0:T(8,128)(2,1)S(1)} collective-permute-done((bf16[17,16,128]{2,1,0:T(8,128)(2,1)S(1)}, bf16[17,16,128]{2,1,0:T(8,128)(2,1)S(1)}, u32[]{:S(2)}, u32[]{:S(2)}) %collective-permute-start) | collective-permute-done | bytes 69664 | tf_op jit(solution)/shard_map/ppermute | solution.py:266
  9.3 2.6 %collective-permute-done.1 = bf16[17,16,128]{2,1,0:T(8,128)(2,1)S(1)} collective-permute-done((bf16[17,16,128]{2,1,0:T(8,128)(2,1)S(1)}, bf16[17,16,128]{2,1,0:T(8,128)(2,1)S(1)}, u32[]{:S(2)}, u32[]{:S(2)}) %collective-permute-start.1) | collective-permute-done | bytes 69664 | tf_op jit(solution)/shard_map/ppermute | solution.py:266
  11.9 1.9 %collective-permute-done.2 = bf16[17,16,128]{2,1,0:T(8,128)(2,1)S(1)} collective-permute-done((bf16[17,16,128]{2,1,0:T(8,128)(2,1)S(1)}, bf16[17,16,128]{2,1,0:T(8,128)(2,1)S(1)}, u32[]{:S(2)}, u32[]{:S(2)}) %collective-permute-start.2) | collective-permute-done | bytes 69664 | tf_op jit(solution)/shard_map/ppermute | solution.py:266
  13.9 2.7 %collective-permute-start.3 = (bf16[17,16,128]{2,1,0:T(8,128)(2,1)S(1)}, bf16[17,16,128]{2,1,0:T(8,128)(2,1)S(1)}, u32[]{:S(2)}, u32[]{:S(2)}) collective-permute-start(bf16[17,16,128]{2,1,0:T(8,128)(2,1)S(1)} %add_convert_fusion.1), channel_id=1, source_target_pairs={{0,16},{4,20},{8,24},{12,28},{16,0},{20,4},{24,8},{28,12},{1,17},{... | collective-permute-start | bytes 208904 | tf_op jit(solution)/shard_map/ppermute | solution.py:266
  16.5 3.2 %collective-permute-done.3 = bf16[17,16,128]{2,1,0:T(8,128)(2,1)S(1)} collective-permute-done((bf16[17,16,128]{2,1,0:T(8,128)(2,1)S(1)}, bf16[17,16,128]{2,1,0:T(8,128)(2,1)S(1)}, u32[]{:S(2)}, u32[]{:S(2)}) %collective-permute-start.3) | collective-permute-done | bytes 69664 | tf_op jit(solution)/shard_map/ppermute | solution.py:266
  19.8 5.8 %all-gather = bf16[68,16,128]{2,1,0:T(8,128)(2,1)S(1)} all-gather(bf16[17,16,128]{2,1,0:T(8,128)(2,1)S(1)} %add_convert_fusion), channel_id=2, replica_groups=mesh['wide'=8,'pair'=4] {'pair'}, dimensions={0}, use_global_device_ids=true | all-gather | bytes 348160 | tf_op jit(solution)/shard_map/all_gather | solution.py:278
  25.6 0.5 %square_product.1 = (f32[64,128]{1,0:T(8,128)S(1)}, f32[64,128]{1,0:T(8,128)S(1)}, bf16[64,128]{1,0:T(8,128)(2,1)S(1)}) custom-call(bf16[4,17,16,128]{3,2,1,0:T(8,128)(2,1)S(1)} %bitcast.4), custom_call_target="tpu_custom_call" | custom-call | tf_op jit(solution)/shard_map/square_product/pallas_call | solution.py:168
  26.1 0.4 %collective-permute-start.6 = (f32[64,128]{1,0:T(8,128)S(1)}, f32[64,128]{1,0:T(8,128)S(1)}, u32[]{:S(2)}, u32[]{:S(2)}) collective-permute-start(f32[64,128]{1,0:T(8,128)S(1)} %get-tuple-element.15.m0), channel_id=1, source_target_pairs={{0,12},{4,8},{8,4},{12,0},{16,28},{20,24},{24,20},{28,16},{1,13},{... | collective-permute-start | bytes 98312 | tf_op jit(solution)/shard_map/ppermute | solution.py:266
  26.5 1.8 %collective-permute-start.5 = (f32[64,128]{1,0:T(8,128)S(1)}, f32[64,128]{1,0:T(8,128)S(1)}, u32[]{:S(2)}, u32[]{:S(2)}) collective-permute-start(f32[64,128]{1,0:T(8,128)S(1)} %get-tuple-element.15.m0), channel_id=1, source_target_pairs={{0,8},{4,12},{8,0},{12,4},{16,24},{20,28},{24,16},{28,20},{1,9},{5... | collective-permute-start | bytes 98312 | tf_op jit(solution)/shard_map/ppermute | solution.py:266
  28.3 1.4 %collective-permute-start.4 = (f32[64,128]{1,0:T(8,128)S(1)}, f32[64,128]{1,0:T(8,128)S(1)}, u32[]{:S(2)}, u32[]{:S(2)}) collective-permute-start(f32[64,128]{1,0:T(8,128)S(1)} %get-tuple-element.15.m0), channel_id=1, source_target_pairs={{0,4},{4,0},{8,12},{12,8},{16,20},{20,16},{24,28},{28,24},{1,5},{5... | collective-permute-start | bytes 98312 | tf_op jit(solution)/shard_map/ppermute | solution.py:266
  29.7 1.4 %collective-permute-done.6.m3 = f32[64,128]{1,0:T(8,128)S(1)} collective-permute-done((f32[64,128]{1,0:T(8,128)S(1)}, f32[64,128]{1,0:T(8,128)S(1)}, u32[]{:S(2)}, u32[]{:S(2)}) %collective-permute-start.6) | collective-permute-done | bytes 32800 | tf_op jit(solution)/shard_map/ppermute | solution.py:266
  31.1 0.0 collective-permute-done.5.m2
  31.1 1.1 %collective-permute-done.4.m1 = f32[64,128]{1,0:T(8,128)S(1)} collective-permute-done((f32[64,128]{1,0:T(8,128)S(1)}, f32[64,128]{1,0:T(8,128)S(1)}, u32[]{:S(2)}, u32[]{:S(2)}) %collective-permute-start.4) | collective-permute-done | bytes 32800 | tf_op jit(solution)/shard_map/ppermute | solution.py:266
  32.2 3.0 %finish.1 = (f32[64,128]{1,0:T(8,128)}, f32[4,64]{1,0:T(4,128)}) custom-call(f32[64,128]{1,0:T(8,128)S(1)} %get-tuple-element.15.m0, f32[64,128]{1,0:T(8,128)S(1)} %collective-permute-done.4.m1, f32[64,128]{1,0:T(8,128)S(1)} %collective-permute-done.5.m2, f32[64,128]{1,0:T(8,128)S(1)} %collective-permute-done.6.m3, f32[64,128]{1,0:T(8,128)S(1)} %get-tuple-element.16.own, ...), custom_call_target="tpu_custom_call" | custom-call | tf_op jit(solution)/shard_map/finish/pallas_call | solution.py:252
  (2 shorter events, 0.1 us)
Async XLA Ops:
  4.0 5.3 %collective-permute-start = (bf16[17,16,128]{2,1,0:T(8,128)(2,1)S(1)}, bf16[17,16,128]{2,1,0:T(8,128)(2,1)S(1)}, u32[]{:S(2)}, u32[]{:S(2)}) collective-permute-start(bf16[17,16,128]{2,1,0:T(8,128)(2,1)S(1)} %get-tuple-element.12), channel_id=1, source_target_pairs={{0,4},{4,0},{8,12},{12,8},{16,20},{20,16},{24,28},{28,24},{1,5},{5... | collective-permute-start | bytes 208904 | tf_op jit(solution)/shard_map/ppermute | solution.py:266
  7.0 4.9 %collective-permute-start.1 = (bf16[17,16,128]{2,1,0:T(8,128)(2,1)S(1)}, bf16[17,16,128]{2,1,0:T(8,128)(2,1)S(1)}, u32[]{:S(2)}, u32[]{:S(2)}) collective-permute-start(bf16[17,16,128]{2,1,0:T(8,128)(2,1)S(1)} %get-tuple-element.13), channel_id=1, source_target_pairs={{0,8},{4,12},{8,0},{12,4},{16,24},{20,28},{24,16},{28,20},{1,9},{5... | collective-permute-start | bytes 208904 | tf_op jit(solution)/shard_map/ppermute | solution.py:266
  8.6 5.2 %collective-permute-start.2 = (bf16[17,16,128]{2,1,0:T(8,128)(2,1)S(1)}, bf16[17,16,128]{2,1,0:T(8,128)(2,1)S(1)}, u32[]{:S(2)}, u32[]{:S(2)}) collective-permute-start(bf16[17,16,128]{2,1,0:T(8,128)(2,1)S(1)} %get-tuple-element.14), channel_id=1, source_target_pairs={{0,12},{4,8},{8,4},{12,0},{16,28},{20,24},{24,20},{28,16},{1,13},{... | collective-permute-start | bytes 208904 | tf_op jit(solution)/shard_map/ppermute | solution.py:266
  13.9 5.9 %collective-permute-start.3 = (bf16[17,16,128]{2,1,0:T(8,128)(2,1)S(1)}, bf16[17,16,128]{2,1,0:T(8,128)(2,1)S(1)}, u32[]{:S(2)}, u32[]{:S(2)}) collective-permute-start(bf16[17,16,128]{2,1,0:T(8,128)(2,1)S(1)} %add_convert_fusion.1), channel_id=1, source_target_pairs={{0,16},{4,20},{8,24},{12,28},{16,0},{20,4},{24,8},{28,12},{1,17},{... | collective-permute-start | bytes 208904 | tf_op jit(solution)/shard_map/ppermute | solution.py:266
  26.1 5.0 %collective-permute-start.6 = (f32[64,128]{1,0:T(8,128)S(1)}, f32[64,128]{1,0:T(8,128)S(1)}, u32[]{:S(2)}, u32[]{:S(2)}) collective-permute-start(f32[64,128]{1,0:T(8,128)S(1)} %get-tuple-element.15.m0), channel_id=1, source_target_pairs={{0,12},{4,8},{8,4},{12,0},{16,28},{20,24},{24,20},{28,16},{1,13},{... | collective-permute-start | bytes 98312 | tf_op jit(solution)/shard_map/ppermute | solution.py:266
  26.5 4.6 %collective-permute-start.5 = (f32[64,128]{1,0:T(8,128)S(1)}, f32[64,128]{1,0:T(8,128)S(1)}, u32[]{:S(2)}, u32[]{:S(2)}) collective-permute-start(f32[64,128]{1,0:T(8,128)S(1)} %get-tuple-element.15.m0), channel_id=1, source_target_pairs={{0,8},{4,12},{8,0},{12,4},{16,24},{20,28},{24,16},{28,20},{1,9},{5... | collective-permute-start | bytes 98312 | tf_op jit(solution)/shard_map/ppermute | solution.py:266
  28.3 3.9 %collective-permute-start.4 = (f32[64,128]{1,0:T(8,128)S(1)}, f32[64,128]{1,0:T(8,128)S(1)}, u32[]{:S(2)}, u32[]{:S(2)}) collective-permute-start(f32[64,128]{1,0:T(8,128)S(1)} %get-tuple-element.15.m0), channel_id=1, source_target_pairs={{0,4},{4,0},{8,12},{12,8},{16,20},{20,16},{24,28},{28,24},{1,5},{5... | collective-permute-start | bytes 98312 | tf_op jit(solution)/shard_map/ppermute | solution.py:266

commit v4 on v3

--- a/solution.py
+++ b/solution.py
@@ -13,6 +13,8 @@
 SQUARE = 4
 CUTS = (2, 2, 2, 2)
 SPLIT = 2
+FIRST = (3, 2, 1)
+SECOND = (1, 2, 3)
 GROUP = 8
 NT = (((1,), (1,)), ((), ()))
 
@@ -268,7 +270,7 @@
 
 def in_squares(blocks, basis_a, basis_b, sketch):
     outs = project(blocks, basis_a.T, basis_b.T, sketch)
-    got = [partner(outs[k], k) for k in range(1, SQUARE)]
+    got = [partner(outs[k], k) for k in FIRST]
     total = outs[0].astype(F32)
     for term in got:
         total = total + term.astype(F32)
@@ -277,7 +279,7 @@
     total = (total.astype(F32) + other.astype(F32)).astype(BF16)
     gathered = lax.all_gather(total, "pair")
     moment, own, turned_sketch = square_product(gathered)
-    moments = [moment] + [partner(moment, k) for k in range(1, SQUARE)]
+    moments = [moment] + [partner(moment, k) for k in SECOND]
     scale = float((basis_a.shape[1] * basis_b.shape[1]) ** 0.5)
     transfer, coefficients = finish(moments, own, turned_sketch, scale, sketch.shape[0])
     return transfer.T, coefficients

time: 35.4 us -> 33.7 us (0.952)
  waiting for transfers between devices: 11 us -> 9.26 us
    ppermute x7, waiting for transfers between devices: 11 us -> 9.26 us  [partner(): lax.ppermute(x, 'wide', [(i, i ^ k) for i in range(lax.axis_size('wide'))])]
  transfers between devices with their start and end apart: 7 -> 7, of which waited for: 6 -> 7; matrix products, arithmetic and copies ran while one was open for 0% -> 0% of each run, Pallas kernels for 0% -> 0%
where the time goes in v4:
time: 33.7 us; the launch traced here: 33.6 us
  starting transfers between devices  10.9 us (32%)
  waiting for transfers between devices  9.26 us (27%)
  Pallas kernels  6.87 us (20%)
  blocking collectives  5.83 us (17%)
  between operations  0.66 us (2%)
    ppermute x7, starting transfers between devices, partner(): lax.ppermute(x, 'wide', [(i, i ^ k) for i in range(lax.axis_size('wide'))])  10.9 us
    ppermute x7, waiting for transfers between devices, partner(): lax.ppermute(x, 'wide', [(i, i ^ k) for i in range(lax.axis_size('wide'))])  9.26 us
    all_gather x1, blocking collectives, in_squares(): gathered = lax.all_gather(total, 'pair')  5.83 us
    pallas_call x1, Pallas kernels, project(): pl.pallas_call(project_kernel, out_shape=[out] * SQUARE, in_specs=[outsid...  3.38 us
    pallas_call x1, Pallas kernels, finish(): pl.pallas_call(functools.partial(finish_kernel, scale), out_shape=[jax.Sh...  3.01 us
  transfers between devices with their start and end apart: 7, of which 7 were waited for; matrix products, arithmetic and copies ran while one was open for 0% of the time, Pallas kernels for 0%

profile of v4, /device:TPU:0, one launch (start us, length us, event | category | flops | bytes accessed | tf_op | source)
XLA Modules:
  0.0 33.6 jit_solution(8581757629706494972)
XLA Ops:
  0.6 3.4 %project.1 = (bf16[17,16,128]{2,1,0:T(8,128)(2,1)S(1)}, bf16[17,16,128]{2,1,0:T(8,128)(2,1)S(1)}, bf16[17,16,128]{2,1,0:T(8,128)(2,1)S(1)}, bf16[17,16,128]{2,1,0:T(8,128)(2,1)S(1)}) custom-call(bf16[32,128,512]{2,1,0:T(8,128)(2,1)} %blocks.1, bf16[64,1024]{1,0:T(8,128)(2,1)} %bitcast.5, bf16[64,512]{1,0:T(8,128)(2,1)} %bitcast.6, bf16[4,64]{1,0:T(4,128)(2,1)} %sketch.1), custom_call_target="tpu_custom_call" | custom-call | tf_op jit(solution)/shard_map/project/pallas_call | solution.py:115
  4.0 4.0 %collective-permute-start = (bf16[17,16,128]{2,1,0:T(8,128)(2,1)S(1)}, bf16[17,16,128]{2,1,0:T(8,128)(2,1)S(1)}, u32[]{:S(2)}, u32[]{:S(2)}) collective-permute-start(bf16[17,16,128]{2,1,0:T(8,128)(2,1)S(1)} %get-tuple-element.12), channel_id=1, source_target_pairs={{0,12},{4,8},{8,4},{12,0},{16,28},{20,24},{24,20},{28,16},{1,13},{... | collective-permute-start | bytes 208904 | tf_op jit(solution)/shard_map/ppermute | solution.py:268
  8.1 0.5 %collective-permute-start.1 = (bf16[17,16,128]{2,1,0:T(8,128)(2,1)S(1)}, bf16[17,16,128]{2,1,0:T(8,128)(2,1)S(1)}, u32[]{:S(2)}, u32[]{:S(2)}) collective-permute-start(bf16[17,16,128]{2,1,0:T(8,128)(2,1)S(1)} %get-tuple-element.13), channel_id=1, source_target_pairs={{0,8},{4,12},{8,0},{12,4},{16,24},{20,28},{24,16},{28,20},{1,9},{5... | collective-permute-start | bytes 208904 | tf_op jit(solution)/shard_map/ppermute | solution.py:268
  8.5 0.2 collective-permute-start.2
  8.7 1.9 %collective-permute-done = bf16[17,16,128]{2,1,0:T(8,128)(2,1)S(1)} collective-permute-done((bf16[17,16,128]{2,1,0:T(8,128)(2,1)S(1)}, bf16[17,16,128]{2,1,0:T(8,128)(2,1)S(1)}, u32[]{:S(2)}, u32[]{:S(2)}) %collective-permute-start) | collective-permute-done | bytes 69664 | tf_op jit(solution)/shard_map/ppermute | solution.py:268
  10.6 1.8 %collective-permute-done.1 = bf16[17,16,128]{2,1,0:T(8,128)(2,1)S(1)} collective-permute-done((bf16[17,16,128]{2,1,0:T(8,128)(2,1)S(1)}, bf16[17,16,128]{2,1,0:T(8,128)(2,1)S(1)}, u32[]{:S(2)}, u32[]{:S(2)}) %collective-permute-start.1) | collective-permute-done | bytes 69664 | tf_op jit(solution)/shard_map/ppermute | solution.py:268
  12.4 0.5 %collective-permute-done.2 = bf16[17,16,128]{2,1,0:T(8,128)(2,1)S(1)} collective-permute-done((bf16[17,16,128]{2,1,0:T(8,128)(2,1)S(1)}, bf16[17,16,128]{2,1,0:T(8,128)(2,1)S(1)}, u32[]{:S(2)}, u32[]{:S(2)}) %collective-permute-start.2) | collective-permute-done | bytes 69664 | tf_op jit(solution)/shard_map/ppermute | solution.py:268
  12.9 2.7 %collective-permute-start.3 = (bf16[17,16,128]{2,1,0:T(8,128)(2,1)S(1)}, bf16[17,16,128]{2,1,0:T(8,128)(2,1)S(1)}, u32[]{:S(2)}, u32[]{:S(2)}) collective-permute-start(bf16[17,16,128]{2,1,0:T(8,128)(2,1)S(1)} %add_convert_fusion.1), channel_id=1, source_target_pairs={{0,16},{4,20},{8,24},{12,28},{16,0},{20,4},{24,8},{28,12},{1,17},{... | collective-permute-start | bytes 208904 | tf_op jit(solution)/shard_map/ppermute | solution.py:268
  15.5 2.6 %collective-permute-done.3 = bf16[17,16,128]{2,1,0:T(8,128)(2,1)S(1)} collective-permute-done((bf16[17,16,128]{2,1,0:T(8,128)(2,1)S(1)}, bf16[17,16,128]{2,1,0:T(8,128)(2,1)S(1)}, u32[]{:S(2)}, u32[]{:S(2)}) %collective-permute-start.3) | collective-permute-done | bytes 69664 | tf_op jit(solution)/shard_map/ppermute | solution.py:268
  18.2 5.8 %all-gather = bf16[68,16,128]{2,1,0:T(8,128)(2,1)S(1)} all-gather(bf16[17,16,128]{2,1,0:T(8,128)(2,1)S(1)} %add_convert_fusion), channel_id=2, replica_groups=mesh['wide'=8,'pair'=4] {'pair'}, dimensions={0}, use_global_device_ids=true | all-gather | bytes 348160 | tf_op jit(solution)/shard_map/all_gather | solution.py:280
  24.0 0.5 %square_product.1 = (f32[64,128]{1,0:T(8,128)S(1)}, f32[64,128]{1,0:T(8,128)S(1)}, bf16[64,128]{1,0:T(8,128)(2,1)S(1)}) custom-call(bf16[4,17,16,128]{3,2,1,0:T(8,128)(2,1)S(1)} %bitcast.4), custom_call_target="tpu_custom_call" | custom-call | tf_op jit(solution)/shard_map/square_product/pallas_call | solution.py:170
  24.5 1.6 %collective-permute-start.6 = (f32[64,128]{1,0:T(8,128)S(1)}, f32[64,128]{1,0:T(8,128)S(1)}, u32[]{:S(2)}, u32[]{:S(2)}) collective-permute-start(f32[64,128]{1,0:T(8,128)S(1)} %get-tuple-element.15.m0), channel_id=1, source_target_pairs={{0,12},{4,8},{8,4},{12,0},{16,28},{20,24},{24,20},{28,16},{1,13},{... | collective-permute-start | bytes 98312 | tf_op jit(solution)/shard_map/ppermute | solution.py:268
  26.1 0.5 %collective-permute-start.5 = (f32[64,128]{1,0:T(8,128)S(1)}, f32[64,128]{1,0:T(8,128)S(1)}, u32[]{:S(2)}, u32[]{:S(2)}) collective-permute-start(f32[64,128]{1,0:T(8,128)S(1)} %get-tuple-element.15.m0), channel_id=1, source_target_pairs={{0,8},{4,12},{8,0},{12,4},{16,24},{20,28},{24,16},{28,20},{1,9},{5... | collective-permute-start | bytes 98312 | tf_op jit(solution)/shard_map/ppermute | solution.py:268
  26.7 1.4 %collective-permute-start.4 = (f32[64,128]{1,0:T(8,128)S(1)}, f32[64,128]{1,0:T(8,128)S(1)}, u32[]{:S(2)}, u32[]{:S(2)}) collective-permute-start(f32[64,128]{1,0:T(8,128)S(1)} %get-tuple-element.15.m0), channel_id=1, source_target_pairs={{0,4},{4,0},{8,12},{12,8},{16,20},{20,16},{24,28},{28,24},{1,5},{5... | collective-permute-start | bytes 98312 | tf_op jit(solution)/shard_map/ppermute | solution.py:268
  28.0 1.4 %collective-permute-done.6.m3 = f32[64,128]{1,0:T(8,128)S(1)} collective-permute-done((f32[64,128]{1,0:T(8,128)S(1)}, f32[64,128]{1,0:T(8,128)S(1)}, u32[]{:S(2)}, u32[]{:S(2)}) %collective-permute-start.6) | collective-permute-done | bytes 32800 | tf_op jit(solution)/shard_map/ppermute | solution.py:268
  29.4 0.6 %collective-permute-done.5.m2 = f32[64,128]{1,0:T(8,128)S(1)} collective-permute-done((f32[64,128]{1,0:T(8,128)S(1)}, f32[64,128]{1,0:T(8,128)S(1)}, u32[]{:S(2)}, u32[]{:S(2)}) %collective-permute-start.5) | collective-permute-done | bytes 32800 | tf_op jit(solution)/shard_map/ppermute | solution.py:268
  30.0 0.5 %collective-permute-done.4.m1 = f32[64,128]{1,0:T(8,128)S(1)} collective-permute-done((f32[64,128]{1,0:T(8,128)S(1)}, f32[64,128]{1,0:T(8,128)S(1)}, u32[]{:S(2)}, u32[]{:S(2)}) %collective-permute-start.4) | collective-permute-done | bytes 32800 | tf_op jit(solution)/shard_map/ppermute | solution.py:268
  30.6 3.0 %finish.1 = (f32[64,128]{1,0:T(8,128)}, f32[4,64]{1,0:T(4,128)}) custom-call(f32[64,128]{1,0:T(8,128)S(1)} %get-tuple-element.15.m0, f32[64,128]{1,0:T(8,128)S(1)} %collective-permute-done.4.m1, f32[64,128]{1,0:T(8,128)S(1)} %collective-permute-done.5.m2, f32[64,128]{1,0:T(8,128)S(1)} %collective-permute-done.6.m3, f32[64,128]{1,0:T(8,128)S(1)} %get-tuple-element.16.own, ...), custom_call_target="tpu_custom_call" | custom-call | tf_op jit(solution)/shard_map/finish/pallas_call | solution.py:254
  (2 shorter events, 0.1 us)
Async XLA Ops:
  4.0 6.6 %collective-permute-start = (bf16[17,16,128]{2,1,0:T(8,128)(2,1)S(1)}, bf16[17,16,128]{2,1,0:T(8,128)(2,1)S(1)}, u32[]{:S(2)}, u32[]{:S(2)}) collective-permute-start(bf16[17,16,128]{2,1,0:T(8,128)(2,1)S(1)} %get-tuple-element.12), channel_id=1, source_target_pairs={{0,12},{4,8},{8,4},{12,0},{16,28},{20,24},{24,20},{28,16},{1,13},{... | collective-permute-start | bytes 208904 | tf_op jit(solution)/shard_map/ppermute | solution.py:268
  8.1 4.3 %collective-permute-start.1 = (bf16[17,16,128]{2,1,0:T(8,128)(2,1)S(1)}, bf16[17,16,128]{2,1,0:T(8,128)(2,1)S(1)}, u32[]{:S(2)}, u32[]{:S(2)}) collective-permute-start(bf16[17,16,128]{2,1,0:T(8,128)(2,1)S(1)} %get-tuple-element.13), channel_id=1, source_target_pairs={{0,8},{4,12},{8,0},{12,4},{16,24},{20,28},{24,16},{28,20},{1,9},{5... | collective-permute-start | bytes 208904 | tf_op jit(solution)/shard_map/ppermute | solution.py:268
  8.5 4.3 %collective-permute-start.2 = (bf16[17,16,128]{2,1,0:T(8,128)(2,1)S(1)}, bf16[17,16,128]{2,1,0:T(8,128)(2,1)S(1)}, u32[]{:S(2)}, u32[]{:S(2)}) collective-permute-start(bf16[17,16,128]{2,1,0:T(8,128)(2,1)S(1)} %get-tuple-element.14), channel_id=1, source_target_pairs={{0,4},{4,0},{8,12},{12,8},{16,20},{20,16},{24,28},{28,24},{1,5},{5... | collective-permute-start | bytes 208904 | tf_op jit(solution)/shard_map/ppermute | solution.py:268
  12.9 5.3 %collective-permute-start.3 = (bf16[17,16,128]{2,1,0:T(8,128)(2,1)S(1)}, bf16[17,16,128]{2,1,0:T(8,128)(2,1)S(1)}, u32[]{:S(2)}, u32[]{:S(2)}) collective-permute-start(bf16[17,16,128]{2,1,0:T(8,128)(2,1)S(1)} %add_convert_fusion.1), channel_id=1, source_target_pairs={{0,16},{4,20},{8,24},{12,28},{16,0},{20,4},{24,8},{28,12},{1,17},{... | collective-permute-start | bytes 208904 | tf_op jit(solution)/shard_map/ppermute | solution.py:268
  24.5 4.9 %collective-permute-start.6 = (f32[64,128]{1,0:T(8,128)S(1)}, f32[64,128]{1,0:T(8,128)S(1)}, u32[]{:S(2)}, u32[]{:S(2)}) collective-permute-start(f32[64,128]{1,0:T(8,128)S(1)} %get-tuple-element.15.m0), channel_id=1, source_target_pairs={{0,12},{4,8},{8,4},{12,0},{16,28},{20,24},{24,20},{28,16},{1,13},{... | collective-permute-start | bytes 98312 | tf_op jit(solution)/shard_map/ppermute | solution.py:268
  26.1 3.9 %collective-permute-start.5 = (f32[64,128]{1,0:T(8,128)S(1)}, f32[64,128]{1,0:T(8,128)S(1)}, u32[]{:S(2)}, u32[]{:S(2)}) collective-permute-start(f32[64,128]{1,0:T(8,128)S(1)} %get-tuple-element.15.m0), channel_id=1, source_target_pairs={{0,8},{4,12},{8,0},{12,4},{16,24},{20,28},{24,16},{28,20},{1,9},{5... | collective-permute-start | bytes 98312 | tf_op jit(solution)/shard_map/ppermute | solution.py:268
  26.7 3.9 %collective-permute-start.4 = (f32[64,128]{1,0:T(8,128)S(1)}, f32[64,128]{1,0:T(8,128)S(1)}, u32[]{:S(2)}, u32[]{:S(2)}) collective-permute-start(f32[64,128]{1,0:T(8,128)S(1)} %get-tuple-element.15.m0), channel_id=1, source_target_pairs={{0,4},{4,0},{8,12},{12,8},{16,20},{20,16},{24,28},{28,24},{1,5},{5... | collective-permute-start | bytes 98312 | tf_op jit(solution)/shard_map/ppermute | solution.py:268

commit v5 on v4

--- a/solution.py
+++ b/solution.py
@@ -15,6 +15,8 @@
 SPLIT = 2
 FIRST = (3, 2, 1)
 SECOND = (1, 2, 3)
+ACROSS = (3, 2, 1)
+CROSS = 1
 GROUP = 8
 NT = (((1,), (1,)), ((), ()))
 
@@ -132,12 +134,16 @@
     )(*(pltpu.with_memory_space_constraint(x, pltpu.HBM) for x in (blocks, basis_a, basis_b, sketch)))
 
 
-def square_kernel(gathered, moment, own, turned_sketch, held):
-    groups, tiles, pairs, _ = gathered.shape
+def square_kernel(*refs):
+    groups = len(refs) - 5
+    moment, own, turned_sketch, gathered, held = refs[groups:]
+    _, tiles, pairs, _ = gathered.shape
     count = tiles - 1
     rank = LANES // 2
     wide = lax.axis_index("wide")
     pair = lax.axis_index("pair")
+    for k in range(groups):
+        gathered[pair ^ k] = refs[k][...]
 
     def tile(p):
         return gathered[:, p].reshape(groups * pairs, LANES)
@@ -162,20 +168,23 @@
     own[...] = held[lax.div(wide, SQUARE) * groups + pair]
 
 
-def square_product(gathered):
-    groups, tiles, pairs, _ = gathered.shape
+def square_product(*groups):
+    tiles, pairs, _ = groups[0].shape
     rank = LANES // 2
     vmem = pl.BlockSpec(memory_space=pltpu.VMEM)
     whole = jax.ShapeDtypeStruct((rank, LANES), F32)
     return pl.pallas_call(
         square_kernel,
         out_shape=[whole, whole, jax.ShapeDtypeStruct((rank, LANES), BF16)],
-        in_specs=[vmem],
+        in_specs=[vmem] * len(groups),
         out_specs=[vmem] * 3,
-        scratch_shapes=[pltpu.VMEM(((tiles - 1) // 2, rank, LANES), F32)],
+        scratch_shapes=[
+            pltpu.VMEM((len(groups),) + groups[0].shape, BF16),
+            pltpu.VMEM(((tiles - 1) // 2, rank, LANES), F32),
+        ],
         compiler_params=pltpu.CompilerParams(vmem_limit_bytes=32 * 2**20),
         name="square_product",
-    )(gathered)
+    )(*groups)
 
 
 def inverse_factor(table):
@@ -235,7 +244,7 @@
     column = lax.broadcasted_iota(jnp.int32, (rank, rank), 1)
     inverse = inverse_factor(jnp.concatenate([gram, (row == column).astype(F32)], axis=1))
     transfer[...] = scale * jnp.dot(
-        inverse, own[...], preferred_element_type=F32, precision=lax.Precision.HIGHEST
+        inverse, own[...], preferred_element_type=F32, precision=lax.Precision.HIGH
     )
     count = coefficients.shape[0]
     groups = lax.axis_size("pair")
@@ -244,7 +253,7 @@
     at = lax.rem(j, 2) * (fibres // 2) + pair * per_group + wide * (count // 2) + lax.div(j, 2)
     pick = (lax.broadcasted_iota(jnp.int32, (8, fibres), 1) == at).astype(F32)
     mine = lax.dot_general(pick, moment, NT, preferred_element_type=F32, precision=lax.Precision.HIGHEST)
-    found = lax.dot_general(mine, inverse, NT, preferred_element_type=F32, precision=lax.Precision.HIGHEST)
+    found = lax.dot_general(mine, inverse, NT, preferred_element_type=F32, precision=lax.Precision.HIGH)
     coefficients[...] = found[:count]
 
 
@@ -268,6 +277,12 @@
     return lax.ppermute(x, "wide", [(i, i ^ k) for i in range(lax.axis_size("wide"))])
 
 
+def beside(x, k, j):
+    wide, pair = lax.axis_size("wide"), lax.axis_size("pair")
+    pairs = [(i * pair + g, (i ^ k) * pair + (g ^ j)) for i in range(wide) for g in range(pair)]
+    return lax.ppermute(x, ("wide", "pair"), pairs)
+
+
 def in_squares(blocks, basis_a, basis_b, sketch):
     outs = project(blocks, basis_a.T, basis_b.T, sketch)
     got = [partner(outs[k], k) for k in FIRST]
@@ -277,9 +292,9 @@
     total = total.astype(BF16)
     other = partner(total, SQUARE)
     total = (total.astype(F32) + other.astype(F32)).astype(BF16)
-    gathered = lax.all_gather(total, "pair")
-    moment, own, turned_sketch = square_product(gathered)
-    moments = [moment] + [partner(moment, k) for k in SECOND]
+    groups = {0: total} | {k: beside(total, 0, k) for k in ACROSS}
+    moment, own, turned_sketch = square_product(*(groups[k] for k in range(len(groups))))
+    moments = [moment] + [beside(moment, k, CROSS) for k in SECOND]
     scale = float((basis_a.shape[1] * basis_b.shape[1]) ** 0.5)
     transfer, coefficients = finish(moments, own, turned_sketch, scale, sketch.shape[0])
     return transfer.T, coefficients

time: 33.7 us -> 32.9 us (0.976)
  blocking collectives: 5.83 us -> 0 us
  waiting for transfers between devices: 9.26 us -> 13.1 us
  starting transfers between devices: 10.9 us -> 12.2 us
    ppermute x0 -> x6, waiting for transfers between devices: none -> 6.4 us  [beside(): return lax.ppermute(x, ('wide', 'pair'), pairs)]
    all_gather x1 -> x0, blocking collectives: 5.83 us -> none  [in_squares(): gathered = lax.all_gather(total, 'pair')]
    ppermute x0 -> x6, starting transfers between devices: none -> 4.87 us  [beside(): return lax.ppermute(x, ('wide', 'pair'), pairs)]
    ppermute x7 -> x4, starting transfers between devices: 10.9 us -> 7.34 us  [partner(): lax.ppermute(x, 'wide', [(i, i ^ k) for i in range(lax.axis_size('wide'))])]
    ppermute x7 -> x4, waiting for transfers between devices: 9.26 us -> 6.73 us  [partner(): lax.ppermute(x, 'wide', [(i, i ^ k) for i in range(lax.axis_size('wide'))])]
  transfers between devices with their start and end apart: 7 -> 10, of which waited for: 7 -> 9; matrix products, arithmetic and copies ran while one was open for 0% -> 0% of each run, Pallas kernels for 0% -> 0%
where the time goes in v5:
time: 32.9 us; the launch traced here: 32.8 us
  waiting for transfers between devices  13.1 us (40%)
  starting transfers between devices  12.2 us (37%)
  Pallas kernels  6.67 us (20%)
  between operations  0.67 us (2%)
    ppermute x4, starting transfers between devices, partner(): lax.ppermute(x, 'wide', [(i, i ^ k) for i in range(lax.axis_size('wide'))])  7.34 us
    ppermute x4, waiting for transfers between devices, partner(): lax.ppermute(x, 'wide', [(i, i ^ k) for i in range(lax.axis_size('wide'))])  6.73 us
    ppermute x6, waiting for transfers between devices, beside(): return lax.ppermute(x, ('wide', 'pair'), pairs)  6.4 us
    ppermute x6, starting transfers between devices, beside(): return lax.ppermute(x, ('wide', 'pair'), pairs)  4.87 us
    pallas_call x1, Pallas kernels, project(): pl.pallas_call(project_kernel, out_shape=[out] * SQUARE, in_specs=[outsid...  3.38 us
    pallas_call x1, Pallas kernels, finish(): pl.pallas_call(functools.partial(finish_kernel, scale), out_shape=[jax.Sh...  2.78 us
  transfers between devices with their start and end apart: 10, of which 9 were waited for; matrix products, arithmetic and copies ran while one was open for 0% of the time, Pallas kernels for 0%

profile of v5, /device:TPU:0, one launch (start us, length us, event | category | flops | bytes accessed | tf_op | source)
XLA Modules:
  0.0 32.8 jit_solution(5090211689395468059)
XLA Ops:
  0.6 3.4 %project.1 = (bf16[17,16,128]{2,1,0:T(8,128)(2,1)S(1)}, bf16[17,16,128]{2,1,0:T(8,128)(2,1)S(1)}, bf16[17,16,128]{2,1,0:T(8,128)(2,1)S(1)}, bf16[17,16,128]{2,1,0:T(8,128)(2,1)S(1)}) custom-call(bf16[32,128,512]{2,1,0:T(8,128)(2,1)} %blocks.1, bf16[64,1024]{1,0:T(8,128)(2,1)} %bitcast.3, bf16[64,512]{1,0:T(8,128)(2,1)} %bitcast.4, bf16[4,64]{1,0:T(4,128)(2,1)} %sketch.1), custom_call_target="tpu_custom_call" | custom-call | tf_op jit(solution)/shard_map/project/pallas_call | solution.py:117
  4.0 4.0 %collective-permute-start = (bf16[17,16,128]{2,1,0:T(8,128)(2,1)S(1)}, bf16[17,16,128]{2,1,0:T(8,128)(2,1)S(1)}, u32[]{:S(2)}, u32[]{:S(2)}) collective-permute-start(bf16[17,16,128]{2,1,0:T(8,128)(2,1)S(1)} %get-tuple-element.12), channel_id=1, source_target_pairs={{0,12},{4,8},{8,4},{12,0},{16,28},{20,24},{24,20},{28,16},{1,13},{... | collective-permute-start | bytes 208904 | tf_op jit(solution)/shard_map/ppermute | solution.py:277
  8.1 0.5 %collective-permute-start.1 = (bf16[17,16,128]{2,1,0:T(8,128)(2,1)S(1)}, bf16[17,16,128]{2,1,0:T(8,128)(2,1)S(1)}, u32[]{:S(2)}, u32[]{:S(2)}) collective-permute-start(bf16[17,16,128]{2,1,0:T(8,128)(2,1)S(1)} %get-tuple-element.13), channel_id=1, source_target_pairs={{0,8},{4,12},{8,0},{12,4},{16,24},{20,28},{24,16},{28,20},{1,9},{5... | collective-permute-start | bytes 208904 | tf_op jit(solution)/shard_map/ppermute | solution.py:277
  8.5 0.2 collective-permute-start.2
  8.7 1.9 %collective-permute-done = bf16[17,16,128]{2,1,0:T(8,128)(2,1)S(1)} collective-permute-done((bf16[17,16,128]{2,1,0:T(8,128)(2,1)S(1)}, bf16[17,16,128]{2,1,0:T(8,128)(2,1)S(1)}, u32[]{:S(2)}, u32[]{:S(2)}) %collective-permute-start) | collective-permute-done | bytes 69664 | tf_op jit(solution)/shard_map/ppermute | solution.py:277
  10.6 1.8 %collective-permute-done.1 = bf16[17,16,128]{2,1,0:T(8,128)(2,1)S(1)} collective-permute-done((bf16[17,16,128]{2,1,0:T(8,128)(2,1)S(1)}, bf16[17,16,128]{2,1,0:T(8,128)(2,1)S(1)}, u32[]{:S(2)}, u32[]{:S(2)}) %collective-permute-start.1) | collective-permute-done | bytes 69664 | tf_op jit(solution)/shard_map/ppermute | solution.py:277
  12.4 0.5 %collective-permute-done.2 = bf16[17,16,128]{2,1,0:T(8,128)(2,1)S(1)} collective-permute-done((bf16[17,16,128]{2,1,0:T(8,128)(2,1)S(1)}, bf16[17,16,128]{2,1,0:T(8,128)(2,1)S(1)}, u32[]{:S(2)}, u32[]{:S(2)}) %collective-permute-start.2) | collective-permute-done | bytes 69664 | tf_op jit(solution)/shard_map/ppermute | solution.py:277
  12.9 2.7 %collective-permute-start.3 = (bf16[17,16,128]{2,1,0:T(8,128)(2,1)S(1)}, bf16[17,16,128]{2,1,0:T(8,128)(2,1)S(1)}, u32[]{:S(2)}, u32[]{:S(2)}) collective-permute-start(bf16[17,16,128]{2,1,0:T(8,128)(2,1)S(1)} %add_convert_fusion.1), channel_id=1, source_target_pairs={{0,16},{4,20},{8,24},{12,28},{16,0},{20,4},{24,8},{28,12},{1,17},{... | collective-permute-start | bytes 208904 | tf_op jit(solution)/shard_map/ppermute | solution.py:277
  15.5 2.6 %collective-permute-done.3 = bf16[17,16,128]{2,1,0:T(8,128)(2,1)S(1)} collective-permute-done((bf16[17,16,128]{2,1,0:T(8,128)(2,1)S(1)}, bf16[17,16,128]{2,1,0:T(8,128)(2,1)S(1)}, u32[]{:S(2)}, u32[]{:S(2)}) %collective-permute-start.3) | collective-permute-done | bytes 69664 | tf_op jit(solution)/shard_map/ppermute | solution.py:277
  18.2 0.1 collective-permute-start.6
  18.2 1.6 %collective-permute-start.5 = (bf16[17,16,128]{2,1,0:T(8,128)(2,1)S(1)}, bf16[17,16,128]{2,1,0:T(8,128)(2,1)S(1)}, u32[]{:S(2)}, u32[]{:S(2)}) collective-permute-start(bf16[17,16,128]{2,1,0:T(8,128)(2,1)S(1)} %add_convert_fusion.refs_0_), channel_id=1, source_target_pairs={{0,2},{1,3},{2,0},{3,1},{4,6},{5,7},{6,4},{7,5},{8,10},{9,11},{10,... | collective-permute-start | bytes 208904 | tf_op jit(solution)/shard_map/ppermute | solution.py:283
  19.8 0.3 collective-permute-start.4
  20.1 2.6 %collective-permute-done.6.refs_3_ = bf16[17,16,128]{2,1,0:T(8,128)(2,1)S(1)} collective-permute-done((bf16[17,16,128]{2,1,0:T(8,128)(2,1)S(1)}, bf16[17,16,128]{2,1,0:T(8,128)(2,1)S(1)}, u32[]{:S(2)}, u32[]{:S(2)}) %collective-permute-start.6) | collective-permute-done | bytes 69664 | tf_op jit(solution)/shard_map/ppermute | solution.py:283
  22.7 1.5 %collective-permute-done.5.refs_2_ = bf16[17,16,128]{2,1,0:T(8,128)(2,1)S(1)} collective-permute-done((bf16[17,16,128]{2,1,0:T(8,128)(2,1)S(1)}, bf16[17,16,128]{2,1,0:T(8,128)(2,1)S(1)}, u32[]{:S(2)}, u32[]{:S(2)}) %collective-permute-start.5) | collective-permute-done | bytes 69664 | tf_op jit(solution)/shard_map/ppermute | solution.py:283
  24.2 0.0 collective-permute-done.4.refs_1_
  24.2 0.5 %square_product.1 = (f32[64,128]{1,0:T(8,128)S(1)}, f32[64,128]{1,0:T(8,128)S(1)}, bf16[64,128]{1,0:T(8,128)(2,1)S(1)}) custom-call(bf16[17,16,128]{2,1,0:T(8,128)(2,1)S(1)} %add_convert_fusion.refs_0_, bf16[17,16,128]{2,1,0:T(8,128)(2,1)S(1)} %collective-permute-done.4.refs_1_, bf16[17,16,128]{2,1,0:T(8,128)(2,1)S(1)} %collective-permute-done.5.refs_2_, ...), custom_call_target="tpu_custom_call" | custom-call | tf_op jit(solution)/shard_map/square_product/pallas_call | solution.py:176
  24.7 1.3 %collective-permute-start.9 = (f32[64,128]{1,0:T(8,128)S(1)}, f32[64,128]{1,0:T(8,128)S(1)}, u32[]{:S(2)}, u32[]{:S(2)}) collective-permute-start(f32[64,128]{1,0:T(8,128)S(1)} %get-tuple-element.15.m0), channel_id=1, source_target_pairs={{0,13},{1,12},{2,15},{3,14},{4,9},{5,8},{6,11},{7,10},{8,5},{9,4},... | collective-permute-start | bytes 98312 | tf_op jit(solution)/shard_map/ppermute | solution.py:283
  26.0 0.5 %collective-permute-start.8 = (f32[64,128]{1,0:T(8,128)S(1)}, f32[64,128]{1,0:T(8,128)S(1)}, u32[]{:S(2)}, u32[]{:S(2)}) collective-permute-start(f32[64,128]{1,0:T(8,128)S(1)} %get-tuple-element.15.m0), channel_id=1, source_target_pairs={{0,9},{1,8},{2,11},{3,10},{4,13},{5,12},{6,15},{7,14},{8,1},{9,0},... | collective-permute-start | bytes 98312 | tf_op jit(solution)/shard_map/ppermute | solution.py:283
  26.5 1.2 %collective-permute-start.7 = (f32[64,128]{1,0:T(8,128)S(1)}, f32[64,128]{1,0:T(8,128)S(1)}, u32[]{:S(2)}, u32[]{:S(2)}) collective-permute-start(f32[64,128]{1,0:T(8,128)S(1)} %get-tuple-element.15.m0), channel_id=1, source_target_pairs={{0,5},{1,4},{2,7},{3,6},{4,1},{5,0},{6,3},{7,2},{8,13},{9,12},{10,... | collective-permute-start | bytes 98312 | tf_op jit(solution)/shard_map/ppermute | solution.py:283
  27.7 1.4 %collective-permute-done.9.m3 = f32[64,128]{1,0:T(8,128)S(1)} collective-permute-done((f32[64,128]{1,0:T(8,128)S(1)}, f32[64,128]{1,0:T(8,128)S(1)}, u32[]{:S(2)}, u32[]{:S(2)}) %collective-permute-start.9) | collective-permute-done | bytes 32800 | tf_op jit(solution)/shard_map/ppermute | solution.py:283
  29.1 0.2 collective-permute-done.8.m2
  29.4 0.6 %collective-permute-done.7.m1 = f32[64,128]{1,0:T(8,128)S(1)} collective-permute-done((f32[64,128]{1,0:T(8,128)S(1)}, f32[64,128]{1,0:T(8,128)S(1)}, u32[]{:S(2)}, u32[]{:S(2)}) %collective-permute-start.7) | collective-permute-done | bytes 32800 | tf_op jit(solution)/shard_map/ppermute | solution.py:283
  30.0 2.8 %finish.1 = (f32[64,128]{1,0:T(8,128)}, f32[4,64]{1,0:T(4,128)}) custom-call(f32[64,128]{1,0:T(8,128)S(1)} %get-tuple-element.15.m0, f32[64,128]{1,0:T(8,128)S(1)} %collective-permute-done.7.m1, f32[64,128]{1,0:T(8,128)S(1)} %collective-permute-done.8.m2, f32[64,128]{1,0:T(8,128)S(1)} %collective-permute-done.9.m3, f32[64,128]{1,0:T(8,128)S(1)} %get-tuple-element.16.own, ...), custom_call_target="tpu_custom_call" | custom-call | tf_op jit(solution)/shard_map/finish/pallas_call | solution.py:263
  (2 shorter events, 0.1 us)
Async XLA Ops:
  4.0 6.6 %collective-permute-start = (bf16[17,16,128]{2,1,0:T(8,128)(2,1)S(1)}, bf16[17,16,128]{2,1,0:T(8,128)(2,1)S(1)}, u32[]{:S(2)}, u32[]{:S(2)}) collective-permute-start(bf16[17,16,128]{2,1,0:T(8,128)(2,1)S(1)} %get-tuple-element.12), channel_id=1, source_target_pairs={{0,12},{4,8},{8,4},{12,0},{16,28},{20,24},{24,20},{28,16},{1,13},{... | collective-permute-start | bytes 208904 | tf_op jit(solution)/shard_map/ppermute | solution.py:277
  8.1 4.3 %collective-permute-start.1 = (bf16[17,16,128]{2,1,0:T(8,128)(2,1)S(1)}, bf16[17,16,128]{2,1,0:T(8,128)(2,1)S(1)}, u32[]{:S(2)}, u32[]{:S(2)}) collective-permute-start(bf16[17,16,128]{2,1,0:T(8,128)(2,1)S(1)} %get-tuple-element.13), channel_id=1, source_target_pairs={{0,8},{4,12},{8,0},{12,4},{16,24},{20,28},{24,16},{28,20},{1,9},{5... | collective-permute-start | bytes 208904 | tf_op jit(solution)/shard_map/ppermute | solution.py:277
  8.5 4.3 %collective-permute-start.2 = (bf16[17,16,128]{2,1,0:T(8,128)(2,1)S(1)}, bf16[17,16,128]{2,1,0:T(8,128)(2,1)S(1)}, u32[]{:S(2)}, u32[]{:S(2)}) collective-permute-start(bf16[17,16,128]{2,1,0:T(8,128)(2,1)S(1)} %get-tuple-element.14), channel_id=1, source_target_pairs={{0,4},{4,0},{8,12},{12,8},{16,20},{20,16},{24,28},{28,24},{1,5},{5... | collective-permute-start | bytes 208904 | tf_op jit(solution)/shard_map/ppermute | solution.py:277
  12.9 5.3 %collective-permute-start.3 = (bf16[17,16,128]{2,1,0:T(8,128)(2,1)S(1)}, bf16[17,16,128]{2,1,0:T(8,128)(2,1)S(1)}, u32[]{:S(2)}, u32[]{:S(2)}) collective-permute-start(bf16[17,16,128]{2,1,0:T(8,128)(2,1)S(1)} %add_convert_fusion.1), channel_id=1, source_target_pairs={{0,16},{4,20},{8,24},{12,28},{16,0},{20,4},{24,8},{28,12},{1,17},{... | collective-permute-start | bytes 208904 | tf_op jit(solution)/shard_map/ppermute | solution.py:277
  18.2 4.5 %collective-permute-start.6 = (bf16[17,16,128]{2,1,0:T(8,128)(2,1)S(1)}, bf16[17,16,128]{2,1,0:T(8,128)(2,1)S(1)}, u32[]{:S(2)}, u32[]{:S(2)}) collective-permute-start(bf16[17,16,128]{2,1,0:T(8,128)(2,1)S(1)} %add_convert_fusion.refs_0_), channel_id=1, source_target_pairs={{0,3},{1,2},{2,1},{3,0},{4,7},{5,6},{6,5},{7,4},{8,11},{9,10},{10,... | collective-permute-start | bytes 208904 | tf_op jit(solution)/shard_map/ppermute | solution.py:283
  18.2 6.0 %collective-permute-start.5 = (bf16[17,16,128]{2,1,0:T(8,128)(2,1)S(1)}, bf16[17,16,128]{2,1,0:T(8,128)(2,1)S(1)}, u32[]{:S(2)}, u32[]{:S(2)}) collective-permute-start(bf16[17,16,128]{2,1,0:T(8,128)(2,1)S(1)} %add_convert_fusion.refs_0_), channel_id=1, source_target_pairs={{0,2},{1,3},{2,0},{3,1},{4,6},{5,7},{6,4},{7,5},{8,10},{9,11},{10,... | collective-permute-start | bytes 208904 | tf_op jit(solution)/shard_map/ppermute | solution.py:283
  19.8 4.4 %collective-permute-start.4 = (bf16[17,16,128]{2,1,0:T(8,128)(2,1)S(1)}, bf16[17,16,128]{2,1,0:T(8,128)(2,1)S(1)}, u32[]{:S(2)}, u32[]{:S(2)}) collective-permute-start(bf16[17,16,128]{2,1,0:T(8,128)(2,1)S(1)} %add_convert_fusion.refs_0_), channel_id=1, source_target_pairs={{0,1},{1,0},{2,3},{3,2},{4,5},{5,4},{6,7},{7,6},{8,9},{9,8},{10,11... | collective-permute-start | bytes 208904 | tf_op jit(solution)/shard_map/ppermute | solution.py:283
  24.7 4.4 %collective-permute-start.9 = (f32[64,128]{1,0:T(8,128)S(1)}, f32[64,128]{1,0:T(8,128)S(1)}, u32[]{:S(2)}, u32[]{:S(2)}) collective-permute-start(f32[64,128]{1,0:T(8,128)S(1)} %get-tuple-element.15.m0), channel_id=1, source_target_pairs={{0,13},{1,12},{2,15},{3,14},{4,9},{5,8},{6,11},{7,10},{8,5},{9,4},... | collective-permute-start | bytes 98312 | tf_op jit(solution)/shard_map/ppermute | solution.py:283
  26.0 3.3 %collective-permute-start.8 = (f32[64,128]{1,0:T(8,128)S(1)}, f32[64,128]{1,0:T(8,128)S(1)}, u32[]{:S(2)}, u32[]{:S(2)}) collective-permute-start(f32[64,128]{1,0:T(8,128)S(1)} %get-tuple-element.15.m0), channel_id=1, source_target_pairs={{0,9},{1,8},{2,11},{3,10},{4,13},{5,12},{6,15},{7,14},{8,1},{9,0},... | collective-permute-start | bytes 98312 | tf_op jit(solution)/shard_map/ppermute | solution.py:283
  26.5 3.5 %collective-permute-start.7 = (f32[64,128]{1,0:T(8,128)S(1)}, f32[64,128]{1,0:T(8,128)S(1)}, u32[]{:S(2)}, u32[]{:S(2)}) collective-permute-start(f32[64,128]{1,0:T(8,128)S(1)} %get-tuple-element.15.m0), channel_id=1, source_target_pairs={{0,5},{1,4},{2,7},{3,6},{4,1},{5,0},{6,3},{7,2},{8,13},{9,12},{10,... | collective-permute-start | bytes 98312 | tf_op jit(solution)/shard_map/ppermute | solution.py:283

commit v6 on v5

--- a/solution.py
+++ b/solution.py
@@ -15,8 +15,6 @@
 SPLIT = 2
 FIRST = (3, 2, 1)
 SECOND = (1, 2, 3)
-ACROSS = (3, 2, 1)
-CROSS = 1
 GROUP = 8
 NT = (((1,), (1,)), ((), ()))
 
@@ -292,9 +290,11 @@
     total = total.astype(BF16)
     other = partner(total, SQUARE)
     total = (total.astype(F32) + other.astype(F32)).astype(BF16)
-    groups = {0: total} | {k: beside(total, 0, k) for k in ACROSS}
-    moment, own, turned_sketch = square_product(*(groups[k] for k in range(len(groups))))
-    moments = [moment] + [beside(moment, k, CROSS) for k in SECOND]
+    across = beside(total, 0, 2)
+    near = beside(total, 0, 1)
+    groups = [total, near, across, beside(across, 0, 1)]
+    moment, own, turned_sketch = square_product(*groups)
+    moments = [moment] + [beside(moment, k, 1) for k in SECOND]
     scale = float((basis_a.shape[1] * basis_b.shape[1]) ** 0.5)
     transfer, coefficients = finish(moments, own, turned_sketch, scale, sketch.shape[0])
     return transfer.T, coefficients

time: 32.9 us -> 32.4 us (0.985)
  no operation moved by 1% of the time
where the time goes in v6:
time: 32.4 us; the launch traced here: 32.2 us
  waiting for transfers between devices  12.9 us (40%)
  starting transfers between devices  11.9 us (37%)
  Pallas kernels  6.67 us (21%)
  between operations  0.66 us (2%)
    ppermute x4, starting transfers between devices, partner(): lax.ppermute(x, 'wide', [(i, i ^ k) for i in range(lax.axis_size('wide'))])  7.34 us
    ppermute x4, waiting for transfers between devices, partner(): lax.ppermute(x, 'wide', [(i, i ^ k) for i in range(lax.axis_size('wide'))])  6.73 us
    ppermute x6, waiting for transfers between devices, beside(): return lax.ppermute(x, ('wide', 'pair'), pairs)  6.17 us
    ppermute x6, starting transfers between devices, beside(): return lax.ppermute(x, ('wide', 'pair'), pairs)  4.59 us
    pallas_call x1, Pallas kernels, project(): pl.pallas_call(project_kernel, out_shape=[out] * SQUARE, in_specs=[outsid...  3.38 us
    pallas_call x1, Pallas kernels, finish(): pl.pallas_call(functools.partial(finish_kernel, scale), out_shape=[jax.Sh...  2.78 us
  transfers between devices with their start and end apart: 10, of which 9 were waited for; matrix products, arithmetic and copies ran while one was open for 0% of the time, Pallas kernels for 0%

profile of v6, /device:TPU:0, one launch (start us, length us, event | category | flops | bytes accessed | tf_op | source)
XLA Modules:
  0.0 32.2 jit_solution(14747393553049070069)
XLA Ops:
  0.6 3.4 %project.1 = (bf16[17,16,128]{2,1,0:T(8,128)(2,1)S(1)}, bf16[17,16,128]{2,1,0:T(8,128)(2,1)S(1)}, bf16[17,16,128]{2,1,0:T(8,128)(2,1)S(1)}, bf16[17,16,128]{2,1,0:T(8,128)(2,1)S(1)}) custom-call(bf16[32,128,512]{2,1,0:T(8,128)(2,1)} %blocks.1, bf16[64,1024]{1,0:T(8,128)(2,1)} %bitcast.3, bf16[64,512]{1,0:T(8,128)(2,1)} %bitcast.4, bf16[4,64]{1,0:T(4,128)(2,1)} %sketch.1), custom_call_target="tpu_custom_call" | custom-call | tf_op jit(solution)/shard_map/project/pallas_call | solution.py:115
  4.0 4.0 %collective-permute-start = (bf16[17,16,128]{2,1,0:T(8,128)(2,1)S(1)}, bf16[17,16,128]{2,1,0:T(8,128)(2,1)S(1)}, u32[]{:S(2)}, u32[]{:S(2)}) collective-permute-start(bf16[17,16,128]{2,1,0:T(8,128)(2,1)S(1)} %get-tuple-element.12), channel_id=1, source_target_pairs={{0,12},{4,8},{8,4},{12,0},{16,28},{20,24},{24,20},{28,16},{1,13},{... | collective-permute-start | bytes 208904 | tf_op jit(solution)/shard_map/ppermute | solution.py:275
  8.1 0.5 %collective-permute-start.1 = (bf16[17,16,128]{2,1,0:T(8,128)(2,1)S(1)}, bf16[17,16,128]{2,1,0:T(8,128)(2,1)S(1)}, u32[]{:S(2)}, u32[]{:S(2)}) collective-permute-start(bf16[17,16,128]{2,1,0:T(8,128)(2,1)S(1)} %get-tuple-element.13), channel_id=1, source_target_pairs={{0,8},{4,12},{8,0},{12,4},{16,24},{20,28},{24,16},{28,20},{1,9},{5... | collective-permute-start | bytes 208904 | tf_op jit(solution)/shard_map/ppermute | solution.py:275
  8.5 0.2 collective-permute-start.2
  8.7 1.9 %collective-permute-done = bf16[17,16,128]{2,1,0:T(8,128)(2,1)S(1)} collective-permute-done((bf16[17,16,128]{2,1,0:T(8,128)(2,1)S(1)}, bf16[17,16,128]{2,1,0:T(8,128)(2,1)S(1)}, u32[]{:S(2)}, u32[]{:S(2)}) %collective-permute-start) | collective-permute-done | bytes 69664 | tf_op jit(solution)/shard_map/ppermute | solution.py:275
  10.6 1.8 %collective-permute-done.1 = bf16[17,16,128]{2,1,0:T(8,128)(2,1)S(1)} collective-permute-done((bf16[17,16,128]{2,1,0:T(8,128)(2,1)S(1)}, bf16[17,16,128]{2,1,0:T(8,128)(2,1)S(1)}, u32[]{:S(2)}, u32[]{:S(2)}) %collective-permute-start.1) | collective-permute-done | bytes 69664 | tf_op jit(solution)/shard_map/ppermute | solution.py:275
  12.4 0.5 %collective-permute-done.2 = bf16[17,16,128]{2,1,0:T(8,128)(2,1)S(1)} collective-permute-done((bf16[17,16,128]{2,1,0:T(8,128)(2,1)S(1)}, bf16[17,16,128]{2,1,0:T(8,128)(2,1)S(1)}, u32[]{:S(2)}, u32[]{:S(2)}) %collective-permute-start.2) | collective-permute-done | bytes 69664 | tf_op jit(solution)/shard_map/ppermute | solution.py:275
  12.9 2.7 %collective-permute-start.3 = (bf16[17,16,128]{2,1,0:T(8,128)(2,1)S(1)}, bf16[17,16,128]{2,1,0:T(8,128)(2,1)S(1)}, u32[]{:S(2)}, u32[]{:S(2)}) collective-permute-start(bf16[17,16,128]{2,1,0:T(8,128)(2,1)S(1)} %add_convert_fusion.1), channel_id=1, source_target_pairs={{0,16},{4,20},{8,24},{12,28},{16,0},{20,4},{24,8},{28,12},{1,17},{... | collective-permute-start | bytes 208904 | tf_op jit(solution)/shard_map/ppermute | solution.py:275
  15.5 2.6 %collective-permute-done.3 = bf16[17,16,128]{2,1,0:T(8,128)(2,1)S(1)} collective-permute-done((bf16[17,16,128]{2,1,0:T(8,128)(2,1)S(1)}, bf16[17,16,128]{2,1,0:T(8,128)(2,1)S(1)}, u32[]{:S(2)}, u32[]{:S(2)}) %collective-permute-start.3) | collective-permute-done | bytes 69664 | tf_op jit(solution)/shard_map/ppermute | solution.py:275
  18.2 1.6 %collective-permute-start.5 = (bf16[17,16,128]{2,1,0:T(8,128)(2,1)S(1)}, bf16[17,16,128]{2,1,0:T(8,128)(2,1)S(1)}, u32[]{:S(2)}, u32[]{:S(2)}) collective-permute-start(bf16[17,16,128]{2,1,0:T(8,128)(2,1)S(1)} %add_convert_fusion.refs_0_), channel_id=1, source_target_pairs={{0,2},{1,3},{2,0},{3,1},{4,6},{5,7},{6,4},{7,5},{8,10},{9,11},{10,... | collective-permute-start | bytes 208904 | tf_op jit(solution)/shard_map/ppermute | solution.py:281
  19.7 0.0 collective-permute-start.4
  19.7 2.8 %collective-permute-done.5.refs_2_ = bf16[17,16,128]{2,1,0:T(8,128)(2,1)S(1)} collective-permute-done((bf16[17,16,128]{2,1,0:T(8,128)(2,1)S(1)}, bf16[17,16,128]{2,1,0:T(8,128)(2,1)S(1)}, u32[]{:S(2)}, u32[]{:S(2)}) %collective-permute-start.5) | collective-permute-done | bytes 69664 | tf_op jit(solution)/shard_map/ppermute | solution.py:281
  22.5 0.0 collective-permute-start.6
  22.5 0.0 collective-permute-done.4.refs_1_
  22.6 1.3 %collective-permute-done.6.refs_3_ = bf16[17,16,128]{2,1,0:T(8,128)(2,1)S(1)} collective-permute-done((bf16[17,16,128]{2,1,0:T(8,128)(2,1)S(1)}, bf16[17,16,128]{2,1,0:T(8,128)(2,1)S(1)}, u32[]{:S(2)}, u32[]{:S(2)}) %collective-permute-start.6) | collective-permute-done | bytes 69664 | tf_op jit(solution)/shard_map/ppermute | solution.py:281
  23.8 0.5 %square_product.1 = (f32[64,128]{1,0:T(8,128)S(1)}, f32[64,128]{1,0:T(8,128)S(1)}, bf16[64,128]{1,0:T(8,128)(2,1)S(1)}) custom-call(bf16[17,16,128]{2,1,0:T(8,128)(2,1)S(1)} %add_convert_fusion.refs_0_, bf16[17,16,128]{2,1,0:T(8,128)(2,1)S(1)} %collective-permute-done.4.refs_1_, bf16[17,16,128]{2,1,0:T(8,128)(2,1)S(1)} %collective-permute-done.5.refs_2_, ...), custom_call_target="tpu_custom_call" | custom-call | tf_op jit(solution)/shard_map/square_product/pallas_call | solution.py:174
  24.3 1.4 %collective-permute-start.9 = (f32[64,128]{1,0:T(8,128)S(1)}, f32[64,128]{1,0:T(8,128)S(1)}, u32[]{:S(2)}, u32[]{:S(2)}) collective-permute-start(f32[64,128]{1,0:T(8,128)S(1)} %get-tuple-element.15.m0), channel_id=1, source_target_pairs={{0,13},{1,12},{2,15},{3,14},{4,9},{5,8},{6,11},{7,10},{8,5},{9,4},... | collective-permute-start | bytes 98312 | tf_op jit(solution)/shard_map/ppermute | solution.py:281
  25.7 0.4 %collective-permute-start.8 = (f32[64,128]{1,0:T(8,128)S(1)}, f32[64,128]{1,0:T(8,128)S(1)}, u32[]{:S(2)}, u32[]{:S(2)}) collective-permute-start(f32[64,128]{1,0:T(8,128)S(1)} %get-tuple-element.15.m0), channel_id=1, source_target_pairs={{0,9},{1,8},{2,11},{3,10},{4,13},{5,12},{6,15},{7,14},{8,1},{9,0},... | collective-permute-start | bytes 98312 | tf_op jit(solution)/shard_map/ppermute | solution.py:281
  26.1 1.2 %collective-permute-start.7 = (f32[64,128]{1,0:T(8,128)S(1)}, f32[64,128]{1,0:T(8,128)S(1)}, u32[]{:S(2)}, u32[]{:S(2)}) collective-permute-start(f32[64,128]{1,0:T(8,128)S(1)} %get-tuple-element.15.m0), channel_id=1, source_target_pairs={{0,5},{1,4},{2,7},{3,6},{4,1},{5,0},{6,3},{7,2},{8,13},{9,12},{10,... | collective-permute-start | bytes 98312 | tf_op jit(solution)/shard_map/ppermute | solution.py:281
  27.4 1.3 %collective-permute-done.9.m3 = f32[64,128]{1,0:T(8,128)S(1)} collective-permute-done((f32[64,128]{1,0:T(8,128)S(1)}, f32[64,128]{1,0:T(8,128)S(1)}, u32[]{:S(2)}, u32[]{:S(2)}) %collective-permute-start.9) | collective-permute-done | bytes 32800 | tf_op jit(solution)/shard_map/ppermute | solution.py:281
  28.6 0.4 %collective-permute-done.8.m2 = f32[64,128]{1,0:T(8,128)S(1)} collective-permute-done((f32[64,128]{1,0:T(8,128)S(1)}, f32[64,128]{1,0:T(8,128)S(1)}, u32[]{:S(2)}, u32[]{:S(2)}) %collective-permute-start.8) | collective-permute-done | bytes 32800 | tf_op jit(solution)/shard_map/ppermute | solution.py:281
  29.0 0.4 %collective-permute-done.7.m1 = f32[64,128]{1,0:T(8,128)S(1)} collective-permute-done((f32[64,128]{1,0:T(8,128)S(1)}, f32[64,128]{1,0:T(8,128)S(1)}, u32[]{:S(2)}, u32[]{:S(2)}) %collective-permute-start.7) | collective-permute-done | bytes 32800 | tf_op jit(solution)/shard_map/ppermute | solution.py:281
  29.5 2.8 %finish.1 = (f32[64,128]{1,0:T(8,128)}, f32[4,64]{1,0:T(4,128)}) custom-call(f32[64,128]{1,0:T(8,128)S(1)} %get-tuple-element.15.m0, f32[64,128]{1,0:T(8,128)S(1)} %collective-permute-done.7.m1, f32[64,128]{1,0:T(8,128)S(1)} %collective-permute-done.8.m2, f32[64,128]{1,0:T(8,128)S(1)} %collective-permute-done.9.m3, f32[64,128]{1,0:T(8,128)S(1)} %get-tuple-element.16.own, ...), custom_call_target="tpu_custom_call" | custom-call | tf_op jit(solution)/shard_map/finish/pallas_call | solution.py:261
  (2 shorter events, 0.1 us)
Async XLA Ops:
  4.0 6.6 %collective-permute-start = (bf16[17,16,128]{2,1,0:T(8,128)(2,1)S(1)}, bf16[17,16,128]{2,1,0:T(8,128)(2,1)S(1)}, u32[]{:S(2)}, u32[]{:S(2)}) collective-permute-start(bf16[17,16,128]{2,1,0:T(8,128)(2,1)S(1)} %get-tuple-element.12), channel_id=1, source_target_pairs={{0,12},{4,8},{8,4},{12,0},{16,28},{20,24},{24,20},{28,16},{1,13},{... | collective-permute-start | bytes 208904 | tf_op jit(solution)/shard_map/ppermute | solution.py:275
  8.1 4.3 %collective-permute-start.1 = (bf16[17,16,128]{2,1,0:T(8,128)(2,1)S(1)}, bf16[17,16,128]{2,1,0:T(8,128)(2,1)S(1)}, u32[]{:S(2)}, u32[]{:S(2)}) collective-permute-start(bf16[17,16,128]{2,1,0:T(8,128)(2,1)S(1)} %get-tuple-element.13), channel_id=1, source_target_pairs={{0,8},{4,12},{8,0},{12,4},{16,24},{20,28},{24,16},{28,20},{1,9},{5... | collective-permute-start | bytes 208904 | tf_op jit(solution)/shard_map/ppermute | solution.py:275
  8.5 4.3 %collective-permute-start.2 = (bf16[17,16,128]{2,1,0:T(8,128)(2,1)S(1)}, bf16[17,16,128]{2,1,0:T(8,128)(2,1)S(1)}, u32[]{:S(2)}, u32[]{:S(2)}) collective-permute-start(bf16[17,16,128]{2,1,0:T(8,128)(2,1)S(1)} %get-tuple-element.14), channel_id=1, source_target_pairs={{0,4},{4,0},{8,12},{12,8},{16,20},{20,16},{24,28},{28,24},{1,5},{5... | collective-permute-start | bytes 208904 | tf_op jit(solution)/shard_map/ppermute | solution.py:275
  12.9 5.3 %collective-permute-start.3 = (bf16[17,16,128]{2,1,0:T(8,128)(2,1)S(1)}, bf16[17,16,128]{2,1,0:T(8,128)(2,1)S(1)}, u32[]{:S(2)}, u32[]{:S(2)}) collective-permute-start(bf16[17,16,128]{2,1,0:T(8,128)(2,1)S(1)} %add_convert_fusion.1), channel_id=1, source_target_pairs={{0,16},{4,20},{8,24},{12,28},{16,0},{20,4},{24,8},{28,12},{1,17},{... | collective-permute-start | bytes 208904 | tf_op jit(solution)/shard_map/ppermute | solution.py:275
  18.2 4.4 %collective-permute-start.5 = (bf16[17,16,128]{2,1,0:T(8,128)(2,1)S(1)}, bf16[17,16,128]{2,1,0:T(8,128)(2,1)S(1)}, u32[]{:S(2)}, u32[]{:S(2)}) collective-permute-start(bf16[17,16,128]{2,1,0:T(8,128)(2,1)S(1)} %add_convert_fusion.refs_0_), channel_id=1, source_target_pairs={{0,2},{1,3},{2,0},{3,1},{4,6},{5,7},{6,4},{7,5},{8,10},{9,11},{10,... | collective-permute-start | bytes 208904 | tf_op jit(solution)/shard_map/ppermute | solution.py:281
  19.7 2.8 %collective-permute-start.4 = (bf16[17,16,128]{2,1,0:T(8,128)(2,1)S(1)}, bf16[17,16,128]{2,1,0:T(8,128)(2,1)S(1)}, u32[]{:S(2)}, u32[]{:S(2)}) collective-permute-start(bf16[17,16,128]{2,1,0:T(8,128)(2,1)S(1)} %add_convert_fusion.refs_0_), channel_id=1, source_target_pairs={{0,1},{1,0},{2,3},{3,2},{4,5},{5,4},{6,7},{7,6},{8,9},{9,8},{10,11... | collective-permute-start | bytes 208904 | tf_op jit(solution)/shard_map/ppermute | solution.py:281
  22.5 1.3 %collective-permute-start.6 = (bf16[17,16,128]{2,1,0:T(8,128)(2,1)S(1)}, bf16[17,16,128]{2,1,0:T(8,128)(2,1)S(1)}, u32[]{:S(2)}, u32[]{:S(2)}) collective-permute-start(bf16[17,16,128]{2,1,0:T(8,128)(2,1)S(1)} %collective-permute-done.5.refs_2_), channel_id=1, source_target_pairs={{0,1},{1,0},{2,3},{3,2},{4,5},{5,4},{6,7},{7,6},{8,9},{9,8},{10,11... | collective-permute-start | bytes 208904 | tf_op jit(solution)/shard_map/ppermute | solution.py:281
  24.3 4.3 %collective-permute-start.9 = (f32[64,128]{1,0:T(8,128)S(1)}, f32[64,128]{1,0:T(8,128)S(1)}, u32[]{:S(2)}, u32[]{:S(2)}) collective-permute-start(f32[64,128]{1,0:T(8,128)S(1)} %get-tuple-element.15.m0), channel_id=1, source_target_pairs={{0,13},{1,12},{2,15},{3,14},{4,9},{5,8},{6,11},{7,10},{8,5},{9,4},... | collective-permute-start | bytes 98312 | tf_op jit(solution)/shard_map/ppermute | solution.py:281
  25.7 3.3 %collective-permute-start.8 = (f32[64,128]{1,0:T(8,128)S(1)}, f32[64,128]{1,0:T(8,128)S(1)}, u32[]{:S(2)}, u32[]{:S(2)}) collective-permute-start(f32[64,128]{1,0:T(8,128)S(1)} %get-tuple-element.15.m0), channel_id=1, source_target_pairs={{0,9},{1,8},{2,11},{3,10},{4,13},{5,12},{6,15},{7,14},{8,1},{9,0},... | collective-permute-start | bytes 98312 | tf_op jit(solution)/shard_map/ppermute | solution.py:281
  26.1 3.4 %collective-permute-start.7 = (f32[64,128]{1,0:T(8,128)S(1)}, f32[64,128]{1,0:T(8,128)S(1)}, u32[]{:S(2)}, u32[]{:S(2)}) collective-permute-start(f32[64,128]{1,0:T(8,128)S(1)} %get-tuple-element.15.m0), channel_id=1, source_target_pairs={{0,5},{1,4},{2,7},{3,6},{4,1},{5,0},{6,3},{7,2},{8,13},{9,12},{10,... | collective-permute-start | bytes 98312 | tf_op jit(solution)/shard_map/ppermute | solution.py:281

commit v7 on v6

--- a/solution.py
+++ b/solution.py
@@ -98,8 +98,8 @@
     count = rank_a // SQUARE
     for k in range(SQUARE):
         found = sums[pl.ds(k * count * pairs, count * pairs), :].reshape(count, pairs, LANES)
-        outs[k][pl.ds(0, count)] = found.astype(BF16)
-        outs[k][count] = tile.astype(BF16)
+        outs[k][pl.ds(0, count)] = found.astype(outs[k].dtype)
+        outs[k][count] = tile.astype(outs[k].dtype)
 
 
 def project(blocks, basis_a, basis_b, sketch):
@@ -109,12 +109,13 @@
     pairs = fibres // 2
     wide = lax.axis_size("wide")
     count = rank_a // SQUARE
-    out = jax.ShapeDtypeStruct((count + 1, pairs, LANES), BF16)
+    shape = (count + 1, pairs, LANES)
+    out = [jax.ShapeDtypeStruct(shape, F32 if k == 0 else BF16) for k in range(SQUARE)]
     vmem = pl.BlockSpec(memory_space=pltpu.VMEM)
     outside = pl.BlockSpec(memory_space=pltpu.HBM)
     return pl.pallas_call(
         project_kernel,
-        out_shape=[out] * SQUARE,
+        out_shape=out,
         in_specs=[outside] * 4,
         out_specs=[vmem] * SQUARE,
         scratch_shapes=[
@@ -124,7 +125,7 @@
             pltpu.VMEM(sketch.shape, BF16),
             pltpu.VMEM((2 * columns, 2 * rank_b), BF16),
             pltpu.VMEM((wide // SQUARE, SQUARE, rank_a // wide, rows), F32),
-            pltpu.VMEM((rank_a * pairs, LANES), F32),
+            pltpu.VMEM((rank_a * pairs + pairs, LANES), F32),
             pltpu.SemaphoreType.DMA((3 + len(CUTS),)),
         ],
         compiler_params=pltpu.CompilerParams(vmem_limit_bytes=32 * 2**20),
@@ -284,7 +285,7 @@
 def in_squares(blocks, basis_a, basis_b, sketch):
     outs = project(blocks, basis_a.T, basis_b.T, sketch)
     got = [partner(outs[k], k) for k in FIRST]
-    total = outs[0].astype(F32)
+    total = outs[0]
     for term in got:
         total = total + term.astype(F32)
     total = total.astype(BF16)

time: 32.4 us -> 32.4 us (level)
  no operation moved by 1% of the time
where the time goes in v7:
time: 32.4 us; the launch traced here: 32.2 us
  waiting for transfers between devices  12.9 us (40%)
  starting transfers between devices  11.9 us (37%)
  Pallas kernels  6.67 us (21%)
  between operations  0.66 us (2%)
    ppermute x4, starting transfers between devices, partner(): lax.ppermute(x, 'wide', [(i, i ^ k) for i in range(lax.axis_size('wide'))])  7.34 us
    ppermute x4, waiting for transfers between devices, partner(): lax.ppermute(x, 'wide', [(i, i ^ k) for i in range(lax.axis_size('wide'))])  6.73 us
    ppermute x6, waiting for transfers between devices, beside(): return lax.ppermute(x, ('wide', 'pair'), pairs)  6.17 us
    ppermute x6, starting transfers between devices, beside(): return lax.ppermute(x, ('wide', 'pair'), pairs)  4.59 us
    pallas_call x1, Pallas kernels, project(): pl.pallas_call(project_kernel, out_shape=out, in_specs=[outside] * 4, out...  3.38 us
    pallas_call x1, Pallas kernels, finish(): pl.pallas_call(functools.partial(finish_kernel, scale), out_shape=[jax.Sh...  2.78 us
  transfers between devices with their start and end apart: 10, of which 9 were waited for; matrix products, arithmetic and copies ran while one was open for 0% of the time, Pallas kernels for 0%

profile of v7, /device:TPU:0, one launch (start us, length us, event | category | flops | bytes accessed | tf_op | source)
XLA Modules:
  0.0 32.2 jit_solution(7657146579980721687)
XLA Ops:
  0.6 3.4 %project.1 = (f32[17,16,128]{2,1,0:T(8,128)S(1)}, bf16[17,16,128]{2,1,0:T(8,128)(2,1)S(1)}, bf16[17,16,128]{2,1,0:T(8,128)(2,1)S(1)}, bf16[17,16,128]{2,1,0:T(8,128)(2,1)S(1)}) custom-call(bf16[32,128,512]{2,1,0:T(8,128)(2,1)} %blocks.1, bf16[64,1024]{1,0:T(8,128)(2,1)} %bitcast.3, bf16[64,512]{1,0:T(8,128)(2,1)} %bitcast.4, bf16[4,64]{1,0:T(4,128)(2,1)} %sketch.1), custom_call_target="tpu_custom_call" | custom-call | tf_op jit(solution)/shard_map/project/pallas_call | solution.py:116
  4.0 4.0 %collective-permute-start = (bf16[17,16,128]{2,1,0:T(8,128)(2,1)S(1)}, bf16[17,16,128]{2,1,0:T(8,128)(2,1)S(1)}, u32[]{:S(2)}, u32[]{:S(2)}) collective-permute-start(bf16[17,16,128]{2,1,0:T(8,128)(2,1)S(1)} %get-tuple-element.12), channel_id=1, source_target_pairs={{0,12},{4,8},{8,4},{12,0},{16,28},{20,24},{24,20},{28,16},{1,13},{... | collective-permute-start | bytes 208904 | tf_op jit(solution)/shard_map/ppermute | solution.py:276
  8.1 0.5 %collective-permute-start.1 = (bf16[17,16,128]{2,1,0:T(8,128)(2,1)S(1)}, bf16[17,16,128]{2,1,0:T(8,128)(2,1)S(1)}, u32[]{:S(2)}, u32[]{:S(2)}) collective-permute-start(bf16[17,16,128]{2,1,0:T(8,128)(2,1)S(1)} %get-tuple-element.13), channel_id=1, source_target_pairs={{0,8},{4,12},{8,0},{12,4},{16,24},{20,28},{24,16},{28,20},{1,9},{5... | collective-permute-start | bytes 208904 | tf_op jit(solution)/shard_map/ppermute | solution.py:276
  8.5 0.2 collective-permute-start.2
  8.7 1.9 %collective-permute-done = bf16[17,16,128]{2,1,0:T(8,128)(2,1)S(1)} collective-permute-done((bf16[17,16,128]{2,1,0:T(8,128)(2,1)S(1)}, bf16[17,16,128]{2,1,0:T(8,128)(2,1)S(1)}, u32[]{:S(2)}, u32[]{:S(2)}) %collective-permute-start) | collective-permute-done | bytes 69664 | tf_op jit(solution)/shard_map/ppermute | solution.py:276
  10.6 1.8 %collective-permute-done.1 = bf16[17,16,128]{2,1,0:T(8,128)(2,1)S(1)} collective-permute-done((bf16[17,16,128]{2,1,0:T(8,128)(2,1)S(1)}, bf16[17,16,128]{2,1,0:T(8,128)(2,1)S(1)}, u32[]{:S(2)}, u32[]{:S(2)}) %collective-permute-start.1) | collective-permute-done | bytes 69664 | tf_op jit(solution)/shard_map/ppermute | solution.py:276
  12.4 0.5 %collective-permute-done.2 = bf16[17,16,128]{2,1,0:T(8,128)(2,1)S(1)} collective-permute-done((bf16[17,16,128]{2,1,0:T(8,128)(2,1)S(1)}, bf16[17,16,128]{2,1,0:T(8,128)(2,1)S(1)}, u32[]{:S(2)}, u32[]{:S(2)}) %collective-permute-start.2) | collective-permute-done | bytes 69664 | tf_op jit(solution)/shard_map/ppermute | solution.py:276
  12.9 2.7 %collective-permute-start.3 = (bf16[17,16,128]{2,1,0:T(8,128)(2,1)S(1)}, bf16[17,16,128]{2,1,0:T(8,128)(2,1)S(1)}, u32[]{:S(2)}, u32[]{:S(2)}) collective-permute-start(bf16[17,16,128]{2,1,0:T(8,128)(2,1)S(1)} %add_convert_fusion.1), channel_id=1, source_target_pairs={{0,16},{4,20},{8,24},{12,28},{16,0},{20,4},{24,8},{28,12},{1,17},{... | collective-permute-start | bytes 208904 | tf_op jit(solution)/shard_map/ppermute | solution.py:276
  15.5 2.6 %collective-permute-done.3 = bf16[17,16,128]{2,1,0:T(8,128)(2,1)S(1)} collective-permute-done((bf16[17,16,128]{2,1,0:T(8,128)(2,1)S(1)}, bf16[17,16,128]{2,1,0:T(8,128)(2,1)S(1)}, u32[]{:S(2)}, u32[]{:S(2)}) %collective-permute-start.3) | collective-permute-done | bytes 69664 | tf_op jit(solution)/shard_map/ppermute | solution.py:276
  18.2 1.6 %collective-permute-start.5 = (bf16[17,16,128]{2,1,0:T(8,128)(2,1)S(1)}, bf16[17,16,128]{2,1,0:T(8,128)(2,1)S(1)}, u32[]{:S(2)}, u32[]{:S(2)}) collective-permute-start(bf16[17,16,128]{2,1,0:T(8,128)(2,1)S(1)} %add_convert_fusion.refs_0_), channel_id=1, source_target_pairs={{0,2},{1,3},{2,0},{3,1},{4,6},{5,7},{6,4},{7,5},{8,10},{9,11},{10,... | collective-permute-start | bytes 208904 | tf_op jit(solution)/shard_map/ppermute | solution.py:282
  19.7 0.0 collective-permute-start.4
  19.7 2.8 %collective-permute-done.5.refs_2_ = bf16[17,16,128]{2,1,0:T(8,128)(2,1)S(1)} collective-permute-done((bf16[17,16,128]{2,1,0:T(8,128)(2,1)S(1)}, bf16[17,16,128]{2,1,0:T(8,128)(2,1)S(1)}, u32[]{:S(2)}, u32[]{:S(2)}) %collective-permute-start.5) | collective-permute-done | bytes 69664 | tf_op jit(solution)/shard_map/ppermute | solution.py:282
  22.5 0.0 collective-permute-start.6
  22.6 0.0 collective-permute-done.4.refs_1_
  22.6 1.3 %collective-permute-done.6.refs_3_ = bf16[17,16,128]{2,1,0:T(8,128)(2,1)S(1)} collective-permute-done((bf16[17,16,128]{2,1,0:T(8,128)(2,1)S(1)}, bf16[17,16,128]{2,1,0:T(8,128)(2,1)S(1)}, u32[]{:S(2)}, u32[]{:S(2)}) %collective-permute-start.6) | collective-permute-done | bytes 69664 | tf_op jit(solution)/shard_map/ppermute | solution.py:282
  23.8 0.5 %square_product.1 = (f32[64,128]{1,0:T(8,128)S(1)}, f32[64,128]{1,0:T(8,128)S(1)}, bf16[64,128]{1,0:T(8,128)(2,1)S(1)}) custom-call(bf16[17,16,128]{2,1,0:T(8,128)(2,1)S(1)} %add_convert_fusion.refs_0_, bf16[17,16,128]{2,1,0:T(8,128)(2,1)S(1)} %collective-permute-done.4.refs_1_, bf16[17,16,128]{2,1,0:T(8,128)(2,1)S(1)} %collective-permute-done.5.refs_2_, ...), custom_call_target="tpu_custom_call" | custom-call | tf_op jit(solution)/shard_map/square_product/pallas_call | solution.py:175
  24.3 1.4 %collective-permute-start.9 = (f32[64,128]{1,0:T(8,128)S(1)}, f32[64,128]{1,0:T(8,128)S(1)}, u32[]{:S(2)}, u32[]{:S(2)}) collective-permute-start(f32[64,128]{1,0:T(8,128)S(1)} %get-tuple-element.15.m0), channel_id=1, source_target_pairs={{0,13},{1,12},{2,15},{3,14},{4,9},{5,8},{6,11},{7,10},{8,5},{9,4},... | collective-permute-start | bytes 98312 | tf_op jit(solution)/shard_map/ppermute | solution.py:282
  25.7 0.4 %collective-permute-start.8 = (f32[64,128]{1,0:T(8,128)S(1)}, f32[64,128]{1,0:T(8,128)S(1)}, u32[]{:S(2)}, u32[]{:S(2)}) collective-permute-start(f32[64,128]{1,0:T(8,128)S(1)} %get-tuple-element.15.m0), channel_id=1, source_target_pairs={{0,9},{1,8},{2,11},{3,10},{4,13},{5,12},{6,15},{7,14},{8,1},{9,0},... | collective-permute-start | bytes 98312 | tf_op jit(solution)/shard_map/ppermute | solution.py:282
  26.1 1.3 %collective-permute-start.7 = (f32[64,128]{1,0:T(8,128)S(1)}, f32[64,128]{1,0:T(8,128)S(1)}, u32[]{:S(2)}, u32[]{:S(2)}) collective-permute-start(f32[64,128]{1,0:T(8,128)S(1)} %get-tuple-element.15.m0), channel_id=1, source_target_pairs={{0,5},{1,4},{2,7},{3,6},{4,1},{5,0},{6,3},{7,2},{8,13},{9,12},{10,... | collective-permute-start | bytes 98312 | tf_op jit(solution)/shard_map/ppermute | solution.py:282
  27.4 1.3 %collective-permute-done.9.m3 = f32[64,128]{1,0:T(8,128)S(1)} collective-permute-done((f32[64,128]{1,0:T(8,128)S(1)}, f32[64,128]{1,0:T(8,128)S(1)}, u32[]{:S(2)}, u32[]{:S(2)}) %collective-permute-start.9) | collective-permute-done | bytes 32800 | tf_op jit(solution)/shard_map/ppermute | solution.py:282
  28.6 0.4 %collective-permute-done.8.m2 = f32[64,128]{1,0:T(8,128)S(1)} collective-permute-done((f32[64,128]{1,0:T(8,128)S(1)}, f32[64,128]{1,0:T(8,128)S(1)}, u32[]{:S(2)}, u32[]{:S(2)}) %collective-permute-start.8) | collective-permute-done | bytes 32800 | tf_op jit(solution)/shard_map/ppermute | solution.py:282
  29.0 0.4 %collective-permute-done.7.m1 = f32[64,128]{1,0:T(8,128)S(1)} collective-permute-done((f32[64,128]{1,0:T(8,128)S(1)}, f32[64,128]{1,0:T(8,128)S(1)}, u32[]{:S(2)}, u32[]{:S(2)}) %collective-permute-start.7) | collective-permute-done | bytes 32800 | tf_op jit(solution)/shard_map/ppermute | solution.py:282
  29.5 2.8 %finish.1 = (f32[64,128]{1,0:T(8,128)}, f32[4,64]{1,0:T(4,128)}) custom-call(f32[64,128]{1,0:T(8,128)S(1)} %get-tuple-element.15.m0, f32[64,128]{1,0:T(8,128)S(1)} %collective-permute-done.7.m1, f32[64,128]{1,0:T(8,128)S(1)} %collective-permute-done.8.m2, f32[64,128]{1,0:T(8,128)S(1)} %collective-permute-done.9.m3, f32[64,128]{1,0:T(8,128)S(1)} %get-tuple-element.16.own, ...), custom_call_target="tpu_custom_call" | custom-call | tf_op jit(solution)/shard_map/finish/pallas_call | solution.py:262
  (2 shorter events, 0.1 us)
Async XLA Ops:
  4.0 6.6 %collective-permute-start = (bf16[17,16,128]{2,1,0:T(8,128)(2,1)S(1)}, bf16[17,16,128]{2,1,0:T(8,128)(2,1)S(1)}, u32[]{:S(2)}, u32[]{:S(2)}) collective-permute-start(bf16[17,16,128]{2,1,0:T(8,128)(2,1)S(1)} %get-tuple-element.12), channel_id=1, source_target_pairs={{0,12},{4,8},{8,4},{12,0},{16,28},{20,24},{24,20},{28,16},{1,13},{... | collective-permute-start | bytes 208904 | tf_op jit(solution)/shard_map/ppermute | solution.py:276
  8.1 4.3 %collective-permute-start.1 = (bf16[17,16,128]{2,1,0:T(8,128)(2,1)S(1)}, bf16[17,16,128]{2,1,0:T(8,128)(2,1)S(1)}, u32[]{:S(2)}, u32[]{:S(2)}) collective-permute-start(bf16[17,16,128]{2,1,0:T(8,128)(2,1)S(1)} %get-tuple-element.13), channel_id=1, source_target_pairs={{0,8},{4,12},{8,0},{12,4},{16,24},{20,28},{24,16},{28,20},{1,9},{5... | collective-permute-start | bytes 208904 | tf_op jit(solution)/shard_map/ppermute | solution.py:276
  8.5 4.3 %collective-permute-start.2 = (bf16[17,16,128]{2,1,0:T(8,128)(2,1)S(1)}, bf16[17,16,128]{2,1,0:T(8,128)(2,1)S(1)}, u32[]{:S(2)}, u32[]{:S(2)}) collective-permute-start(bf16[17,16,128]{2,1,0:T(8,128)(2,1)S(1)} %get-tuple-element.14), channel_id=1, source_target_pairs={{0,4},{4,0},{8,12},{12,8},{16,20},{20,16},{24,28},{28,24},{1,5},{5... | collective-permute-start | bytes 208904 | tf_op jit(solution)/shard_map/ppermute | solution.py:276
  12.9 5.3 %collective-permute-start.3 = (bf16[17,16,128]{2,1,0:T(8,128)(2,1)S(1)}, bf16[17,16,128]{2,1,0:T(8,128)(2,1)S(1)}, u32[]{:S(2)}, u32[]{:S(2)}) collective-permute-start(bf16[17,16,128]{2,1,0:T(8,128)(2,1)S(1)} %add_convert_fusion.1), channel_id=1, source_target_pairs={{0,16},{4,20},{8,24},{12,28},{16,0},{20,4},{24,8},{28,12},{1,17},{... | collective-permute-start | bytes 208904 | tf_op jit(solution)/shard_map/ppermute | solution.py:276
  18.2 4.4 %collective-permute-start.5 = (bf16[17,16,128]{2,1,0:T(8,128)(2,1)S(1)}, bf16[17,16,128]{2,1,0:T(8,128)(2,1)S(1)}, u32[]{:S(2)}, u32[]{:S(2)}) collective-permute-start(bf16[17,16,128]{2,1,0:T(8,128)(2,1)S(1)} %add_convert_fusion.refs_0_), channel_id=1, source_target_pairs={{0,2},{1,3},{2,0},{3,1},{4,6},{5,7},{6,4},{7,5},{8,10},{9,11},{10,... | collective-permute-start | bytes 208904 | tf_op jit(solution)/shard_map/ppermute | solution.py:282
  19.7 2.8 %collective-permute-start.4 = (bf16[17,16,128]{2,1,0:T(8,128)(2,1)S(1)}, bf16[17,16,128]{2,1,0:T(8,128)(2,1)S(1)}, u32[]{:S(2)}, u32[]{:S(2)}) collective-permute-start(bf16[17,16,128]{2,1,0:T(8,128)(2,1)S(1)} %add_convert_fusion.refs_0_), channel_id=1, source_target_pairs={{0,1},{1,0},{2,3},{3,2},{4,5},{5,4},{6,7},{7,6},{8,9},{9,8},{10,11... | collective-permute-start | bytes 208904 | tf_op jit(solution)/shard_map/ppermute | solution.py:282
  22.5 1.3 %collective-permute-start.6 = (bf16[17,16,128]{2,1,0:T(8,128)(2,1)S(1)}, bf16[17,16,128]{2,1,0:T(8,128)(2,1)S(1)}, u32[]{:S(2)}, u32[]{:S(2)}) collective-permute-start(bf16[17,16,128]{2,1,0:T(8,128)(2,1)S(1)} %collective-permute-done.5.refs_2_), channel_id=1, source_target_pairs={{0,1},{1,0},{2,3},{3,2},{4,5},{5,4},{6,7},{7,6},{8,9},{9,8},{10,11... | collective-permute-start | bytes 208904 | tf_op jit(solution)/shard_map/ppermute | solution.py:282
  24.3 4.3 %collective-permute-start.9 = (f32[64,128]{1,0:T(8,128)S(1)}, f32[64,128]{1,0:T(8,128)S(1)}, u32[]{:S(2)}, u32[]{:S(2)}) collective-permute-start(f32[64,128]{1,0:T(8,128)S(1)} %get-tuple-element.15.m0), channel_id=1, source_target_pairs={{0,13},{1,12},{2,15},{3,14},{4,9},{5,8},{6,11},{7,10},{8,5},{9,4},... | collective-permute-start | bytes 98312 | tf_op jit(solution)/shard_map/ppermute | solution.py:282
  25.7 3.3 %collective-permute-start.8 = (f32[64,128]{1,0:T(8,128)S(1)}, f32[64,128]{1,0:T(8,128)S(1)}, u32[]{:S(2)}, u32[]{:S(2)}) collective-permute-start(f32[64,128]{1,0:T(8,128)S(1)} %get-tuple-element.15.m0), channel_id=1, source_target_pairs={{0,9},{1,8},{2,11},{3,10},{4,13},{5,12},{6,15},{7,14},{8,1},{9,0},... | collective-permute-start | bytes 98312 | tf_op jit(solution)/shard_map/ppermute | solution.py:282
  26.1 3.3 %collective-permute-start.7 = (f32[64,128]{1,0:T(8,128)S(1)}, f32[64,128]{1,0:T(8,128)S(1)}, u32[]{:S(2)}, u32[]{:S(2)}) collective-permute-start(f32[64,128]{1,0:T(8,128)S(1)} %get-tuple-element.15.m0), channel_id=1, source_target_pairs={{0,5},{1,4},{2,7},{3,6},{4,1},{5,0},{6,3},{7,2},{8,13},{9,12},{10,... | collective-permute-start | bytes 98312 | tf_op jit(solution)/shard_map/ppermute | solution.py:282

commit v8 on v7

--- a/solution.py
+++ b/solution.py
@@ -289,11 +289,12 @@
     for term in got:
         total = total + term.astype(F32)
     total = total.astype(BF16)
-    other = partner(total, SQUARE)
-    total = (total.astype(F32) + other.astype(F32)).astype(BF16)
-    across = beside(total, 0, 2)
-    near = beside(total, 0, 1)
-    groups = [total, near, across, beside(across, 0, 1)]
+    above = beside(total, SQUARE, 0)
+    both = beside(total, SQUARE, 2)
+    level = beside(total, 0, 2)
+    here = (total.astype(F32) + above.astype(F32)).astype(BF16)
+    across = (level.astype(F32) + both.astype(F32)).astype(BF16)
+    groups = [here, beside(here, 0, 1), across, beside(across, 0, 1)]
     moment, own, turned_sketch = square_product(*groups)
     moments = [moment] + [beside(moment, k, 1) for k in SECOND]
     scale = float((basis_a.shape[1] * basis_b.shape[1]) ** 0.5)

time: 32.4 us -> 32.2 us (level)
  waiting for transfers between devices: 12.9 us -> 12.3 us
  starting transfers between devices: 11.9 us -> 12.3 us
    ppermute x6 -> x8, starting transfers between devices: 4.59 us -> 7.63 us  [beside(): return lax.ppermute(x, ('wide', 'pair'), pairs)]
    ppermute x4 -> x3, starting transfers between devices: 7.34 us -> 4.69 us  [partner(): lax.ppermute(x, 'wide', [(i, i ^ k) for i in range(lax.axis_size('wide'))])]
    ppermute x4 -> x3, waiting for transfers between devices: 6.73 us -> 4.12 us  [partner(): lax.ppermute(x, 'wide', [(i, i ^ k) for i in range(lax.axis_size('wide'))])]
    ppermute x6 -> x8, waiting for transfers between devices: 6.17 us -> 8.2 us  [beside(): return lax.ppermute(x, ('wide', 'pair'), pairs)]
  transfers between devices with their start and end apart: 10 -> 11, of which waited for: 9 -> 10; matrix products, arithmetic and copies ran while one was open for 0% -> 0% of each run, Pallas kernels for 0% -> 0%
where the time goes in v8:
time: 32.2 us; the launch traced here: 32.1 us
  starting transfers between devices  12.3 us (38%)
  waiting for transfers between devices  12.3 us (38%)
  Pallas kernels  6.67 us (21%)
  between operations  0.69 us (2%)
    ppermute x8, waiting for transfers between devices, beside(): return lax.ppermute(x, ('wide', 'pair'), pairs)  8.2 us
    ppermute x8, starting transfers between devices, beside(): return lax.ppermute(x, ('wide', 'pair'), pairs)  7.63 us
    ppermute x3, starting transfers between devices, partner(): lax.ppermute(x, 'wide', [(i, i ^ k) for i in range(lax.axis_size('wide'))])  4.69 us
    ppermute x3, waiting for transfers between devices, partner(): lax.ppermute(x, 'wide', [(i, i ^ k) for i in range(lax.axis_size('wide'))])  4.12 us
    pallas_call x1, Pallas kernels, project(): pl.pallas_call(project_kernel, out_shape=out, in_specs=[outside] * 4, out...  3.38 us
    pallas_call x1, Pallas kernels, finish(): pl.pallas_call(functools.partial(finish_kernel, scale), out_shape=[jax.Sh...  2.78 us
  transfers between devices with their start and end apart: 11, of which 10 were waited for; matrix products, arithmetic and copies ran while one was open for 0% of the time, Pallas kernels for 0%

profile of v8, /device:TPU:0, one launch (start us, length us, event | category | flops | bytes accessed | tf_op | source)
XLA Modules:
  0.0 32.1 jit_solution(1606416728283993666)
XLA Ops:
  0.6 3.4 %project.1 = (f32[17,16,128]{2,1,0:T(8,128)S(1)}, bf16[17,16,128]{2,1,0:T(8,128)(2,1)S(1)}, bf16[17,16,128]{2,1,0:T(8,128)(2,1)S(1)}, bf16[17,16,128]{2,1,0:T(8,128)(2,1)S(1)}) custom-call(bf16[32,128,512]{2,1,0:T(8,128)(2,1)} %blocks.1, bf16[64,1024]{1,0:T(8,128)(2,1)} %bitcast.3, bf16[64,512]{1,0:T(8,128)(2,1)} %bitcast.4, bf16[4,64]{1,0:T(4,128)(2,1)} %sketch.1), custom_call_target="tpu_custom_call" | custom-call | tf_op jit(solution)/shard_map/project/pallas_call | solution.py:116
  4.0 4.0 %collective-permute-start = (bf16[17,16,128]{2,1,0:T(8,128)(2,1)S(1)}, bf16[17,16,128]{2,1,0:T(8,128)(2,1)S(1)}, u32[]{:S(2)}, u32[]{:S(2)}) collective-permute-start(bf16[17,16,128]{2,1,0:T(8,128)(2,1)S(1)} %get-tuple-element.12), channel_id=1, source_target_pairs={{0,12},{4,8},{8,4},{12,0},{16,28},{20,24},{24,20},{28,16},{1,13},{... | collective-permute-start | bytes 208904 | tf_op jit(solution)/shard_map/ppermute | solution.py:276
  8.1 0.5 %collective-permute-start.1 = (bf16[17,16,128]{2,1,0:T(8,128)(2,1)S(1)}, bf16[17,16,128]{2,1,0:T(8,128)(2,1)S(1)}, u32[]{:S(2)}, u32[]{:S(2)}) collective-permute-start(bf16[17,16,128]{2,1,0:T(8,128)(2,1)S(1)} %get-tuple-element.13), channel_id=1, source_target_pairs={{0,8},{4,12},{8,0},{12,4},{16,24},{20,28},{24,16},{28,20},{1,9},{5... | collective-permute-start | bytes 208904 | tf_op jit(solution)/shard_map/ppermute | solution.py:276
  8.5 0.2 collective-permute-start.2
  8.7 1.9 %collective-permute-done = bf16[17,16,128]{2,1,0:T(8,128)(2,1)S(1)} collective-permute-done((bf16[17,16,128]{2,1,0:T(8,128)(2,1)S(1)}, bf16[17,16,128]{2,1,0:T(8,128)(2,1)S(1)}, u32[]{:S(2)}, u32[]{:S(2)}) %collective-permute-start) | collective-permute-done | bytes 69664 | tf_op jit(solution)/shard_map/ppermute | solution.py:276
  10.6 1.8 %collective-permute-done.1 = bf16[17,16,128]{2,1,0:T(8,128)(2,1)S(1)} collective-permute-done((bf16[17,16,128]{2,1,0:T(8,128)(2,1)S(1)}, bf16[17,16,128]{2,1,0:T(8,128)(2,1)S(1)}, u32[]{:S(2)}, u32[]{:S(2)}) %collective-permute-start.1) | collective-permute-done | bytes 69664 | tf_op jit(solution)/shard_map/ppermute | solution.py:276
  12.4 0.5 %collective-permute-done.2 = bf16[17,16,128]{2,1,0:T(8,128)(2,1)S(1)} collective-permute-done((bf16[17,16,128]{2,1,0:T(8,128)(2,1)S(1)}, bf16[17,16,128]{2,1,0:T(8,128)(2,1)S(1)}, u32[]{:S(2)}, u32[]{:S(2)}) %collective-permute-start.2) | collective-permute-done | bytes 69664 | tf_op jit(solution)/shard_map/ppermute | solution.py:276
  12.9 3.6 %collective-permute-start.6 = (bf16[17,16,128]{2,1,0:T(8,128)(2,1)S(1)}, bf16[17,16,128]{2,1,0:T(8,128)(2,1)S(1)}, u32[]{:S(2)}, u32[]{:S(2)}) collective-permute-start(bf16[17,16,128]{2,1,0:T(8,128)(2,1)S(1)} %add_convert_fusion.2), channel_id=1, source_target_pairs={{0,18},{1,19},{2,16},{3,17},{4,22},{5,23},{6,20},{7,21},{8,26},{9,... | collective-permute-start | bytes 208904 | tf_op jit(solution)/shard_map/ppermute | solution.py:282
  16.5 0.5 %collective-permute-start.5 = (bf16[17,16,128]{2,1,0:T(8,128)(2,1)S(1)}, bf16[17,16,128]{2,1,0:T(8,128)(2,1)S(1)}, u32[]{:S(2)}, u32[]{:S(2)}) collective-permute-start(bf16[17,16,128]{2,1,0:T(8,128)(2,1)S(1)} %add_convert_fusion.2), channel_id=1, source_target_pairs={{0,2},{1,3},{2,0},{3,1},{4,6},{5,7},{6,4},{7,5},{8,10},{9,11},{10,... | collective-permute-start | bytes 208904 | tf_op jit(solution)/shard_map/ppermute | solution.py:282
  17.0 0.3 %collective-permute-start.3 = (bf16[17,16,128]{2,1,0:T(8,128)(2,1)S(1)}, bf16[17,16,128]{2,1,0:T(8,128)(2,1)S(1)}, u32[]{:S(2)}, u32[]{:S(2)}) collective-permute-start(bf16[17,16,128]{2,1,0:T(8,128)(2,1)S(1)} %add_convert_fusion.2), channel_id=1, source_target_pairs={{0,16},{1,17},{2,18},{3,19},{4,20},{5,21},{6,22},{7,23},{8,24},{9,... | collective-permute-start | bytes 208904 | tf_op jit(solution)/shard_map/ppermute | solution.py:282
  17.3 1.7 %collective-permute-done.6 = bf16[17,16,128]{2,1,0:T(8,128)(2,1)S(1)} collective-permute-done((bf16[17,16,128]{2,1,0:T(8,128)(2,1)S(1)}, bf16[17,16,128]{2,1,0:T(8,128)(2,1)S(1)}, u32[]{:S(2)}, u32[]{:S(2)}) %collective-permute-start.6) | collective-permute-done | bytes 69664 | tf_op jit(solution)/shard_map/ppermute | solution.py:282
  19.0 1.7 %collective-permute-done.5 = bf16[17,16,128]{2,1,0:T(8,128)(2,1)S(1)} collective-permute-done((bf16[17,16,128]{2,1,0:T(8,128)(2,1)S(1)}, bf16[17,16,128]{2,1,0:T(8,128)(2,1)S(1)}, u32[]{:S(2)}, u32[]{:S(2)}) %collective-permute-start.5) | collective-permute-done | bytes 69664 | tf_op jit(solution)/shard_map/ppermute | solution.py:282
  20.8 0.1 collective-permute-start.7
  20.9 1.3 %collective-permute-done.3 = bf16[17,16,128]{2,1,0:T(8,128)(2,1)S(1)} collective-permute-done((bf16[17,16,128]{2,1,0:T(8,128)(2,1)S(1)}, bf16[17,16,128]{2,1,0:T(8,128)(2,1)S(1)}, u32[]{:S(2)}, u32[]{:S(2)}) %collective-permute-start.3) | collective-permute-done | bytes 69664 | tf_op jit(solution)/shard_map/ppermute | solution.py:282
  22.2 0.1 collective-permute-start.4
  22.3 0.0 collective-permute-done.7.refs_3_
  22.3 1.2 %collective-permute-done.4.refs_1_ = bf16[17,16,128]{2,1,0:T(8,128)(2,1)S(1)} collective-permute-done((bf16[17,16,128]{2,1,0:T(8,128)(2,1)S(1)}, bf16[17,16,128]{2,1,0:T(8,128)(2,1)S(1)}, u32[]{:S(2)}, u32[]{:S(2)}) %collective-permute-start.4) | collective-permute-done | bytes 69664 | tf_op jit(solution)/shard_map/ppermute | solution.py:282
  23.6 0.5 %square_product.1 = (f32[64,128]{1,0:T(8,128)S(1)}, f32[64,128]{1,0:T(8,128)S(1)}, bf16[64,128]{1,0:T(8,128)(2,1)S(1)}) custom-call(bf16[17,16,128]{2,1,0:T(8,128)(2,1)S(1)} %add_convert_fusion.1.refs_0_, bf16[17,16,128]{2,1,0:T(8,128)(2,1)S(1)} %collective-permute-done.4.refs_1_, bf16[17,16,128]{2,1,0:T(8,128)(2,1)S(1)} %add_convert_fusion.refs_2_, ...), custom_call_target="tpu_custom_call" | custom-call | tf_op jit(solution)/shard_map/square_product/pallas_call | solution.py:175
  24.1 1.4 %collective-permute-start.10 = (f32[64,128]{1,0:T(8,128)S(1)}, f32[64,128]{1,0:T(8,128)S(1)}, u32[]{:S(2)}, u32[]{:S(2)}) collective-permute-start(f32[64,128]{1,0:T(8,128)S(1)} %get-tuple-element.15.m0), channel_id=1, source_target_pairs={{0,13},{1,12},{2,15},{3,14},{4,9},{5,8},{6,11},{7,10},{8,5},{9,4},... | collective-permute-start | bytes 98312 | tf_op jit(solution)/shard_map/ppermute | solution.py:282
  25.4 0.5 %collective-permute-start.9 = (f32[64,128]{1,0:T(8,128)S(1)}, f32[64,128]{1,0:T(8,128)S(1)}, u32[]{:S(2)}, u32[]{:S(2)}) collective-permute-start(f32[64,128]{1,0:T(8,128)S(1)} %get-tuple-element.15.m0), channel_id=1, source_target_pairs={{0,9},{1,8},{2,11},{3,10},{4,13},{5,12},{6,15},{7,14},{8,1},{9,0},... | collective-permute-start | bytes 98312 | tf_op jit(solution)/shard_map/ppermute | solution.py:282
  26.0 1.1 %collective-permute-start.8 = (f32[64,128]{1,0:T(8,128)S(1)}, f32[64,128]{1,0:T(8,128)S(1)}, u32[]{:S(2)}, u32[]{:S(2)}) collective-permute-start(f32[64,128]{1,0:T(8,128)S(1)} %get-tuple-element.15.m0), channel_id=1, source_target_pairs={{0,5},{1,4},{2,7},{3,6},{4,1},{5,0},{6,3},{7,2},{8,13},{9,12},{10,... | collective-permute-start | bytes 98312 | tf_op jit(solution)/shard_map/ppermute | solution.py:282
  27.1 1.3 %collective-permute-done.10.m3 = f32[64,128]{1,0:T(8,128)S(1)} collective-permute-done((f32[64,128]{1,0:T(8,128)S(1)}, f32[64,128]{1,0:T(8,128)S(1)}, u32[]{:S(2)}, u32[]{:S(2)}) %collective-permute-start.10) | collective-permute-done | bytes 32800 | tf_op jit(solution)/shard_map/ppermute | solution.py:282
  28.4 0.4 %collective-permute-done.9.m2 = f32[64,128]{1,0:T(8,128)S(1)} collective-permute-done((f32[64,128]{1,0:T(8,128)S(1)}, f32[64,128]{1,0:T(8,128)S(1)}, u32[]{:S(2)}, u32[]{:S(2)}) %collective-permute-start.9) | collective-permute-done | bytes 32800 | tf_op jit(solution)/shard_map/ppermute | solution.py:282
  28.8 0.5 %collective-permute-done.8.m1 = f32[64,128]{1,0:T(8,128)S(1)} collective-permute-done((f32[64,128]{1,0:T(8,128)S(1)}, f32[64,128]{1,0:T(8,128)S(1)}, u32[]{:S(2)}, u32[]{:S(2)}) %collective-permute-start.8) | collective-permute-done | bytes 32800 | tf_op jit(solution)/shard_map/ppermute | solution.py:282
  29.3 2.8 %finish.1 = (f32[64,128]{1,0:T(8,128)}, f32[4,64]{1,0:T(4,128)}) custom-call(f32[64,128]{1,0:T(8,128)S(1)} %get-tuple-element.15.m0, f32[64,128]{1,0:T(8,128)S(1)} %collective-permute-done.8.m1, f32[64,128]{1,0:T(8,128)S(1)} %collective-permute-done.9.m2, f32[64,128]{1,0:T(8,128)S(1)} %collective-permute-done.10.m3, f32[64,128]{1,0:T(8,128)S(1)} %get-tuple-element.16.own, ...), custom_call_target="tpu_custom_call" | custom-call | tf_op jit(solution)/shard_map/finish/pallas_call | solution.py:262
  (3 shorter events, 0.1 us)
Async XLA Ops:
  4.0 6.6 %collective-permute-start = (bf16[17,16,128]{2,1,0:T(8,128)(2,1)S(1)}, bf16[17,16,128]{2,1,0:T(8,128)(2,1)S(1)}, u32[]{:S(2)}, u32[]{:S(2)}) collective-permute-start(bf16[17,16,128]{2,1,0:T(8,128)(2,1)S(1)} %get-tuple-element.12), channel_id=1, source_target_pairs={{0,12},{4,8},{8,4},{12,0},{16,28},{20,24},{24,20},{28,16},{1,13},{... | collective-permute-start | bytes 208904 | tf_op jit(solution)/shard_map/ppermute | solution.py:276
  8.1 4.3 %collective-permute-start.1 = (bf16[17,16,128]{2,1,0:T(8,128)(2,1)S(1)}, bf16[17,16,128]{2,1,0:T(8,128)(2,1)S(1)}, u32[]{:S(2)}, u32[]{:S(2)}) collective-permute-start(bf16[17,16,128]{2,1,0:T(8,128)(2,1)S(1)} %get-tuple-element.13), channel_id=1, source_target_pairs={{0,8},{4,12},{8,0},{12,4},{16,24},{20,28},{24,16},{28,20},{1,9},{5... | collective-permute-start | bytes 208904 | tf_op jit(solution)/shard_map/ppermute | solution.py:276
  8.5 4.3 %collective-permute-start.2 = (bf16[17,16,128]{2,1,0:T(8,128)(2,1)S(1)}, bf16[17,16,128]{2,1,0:T(8,128)(2,1)S(1)}, u32[]{:S(2)}, u32[]{:S(2)}) collective-permute-start(bf16[17,16,128]{2,1,0:T(8,128)(2,1)S(1)} %get-tuple-element.14), channel_id=1, source_target_pairs={{0,4},{4,0},{8,12},{12,8},{16,20},{20,16},{24,28},{28,24},{1,5},{5... | collective-permute-start | bytes 208904 | tf_op jit(solution)/shard_map/ppermute | solution.py:276
  12.9 6.2 %collective-permute-start.6 = (bf16[17,16,128]{2,1,0:T(8,128)(2,1)S(1)}, bf16[17,16,128]{2,1,0:T(8,128)(2,1)S(1)}, u32[]{:S(2)}, u32[]{:S(2)}) collective-permute-start(bf16[17,16,128]{2,1,0:T(8,128)(2,1)S(1)} %add_convert_fusion.2), channel_id=1, source_target_pairs={{0,18},{1,19},{2,16},{3,17},{4,22},{5,23},{6,20},{7,21},{8,26},{9,... | collective-permute-start | bytes 208904 | tf_op jit(solution)/shard_map/ppermute | solution.py:282
  16.5 4.3 %collective-permute-start.5 = (bf16[17,16,128]{2,1,0:T(8,128)(2,1)S(1)}, bf16[17,16,128]{2,1,0:T(8,128)(2,1)S(1)}, u32[]{:S(2)}, u32[]{:S(2)}) collective-permute-start(bf16[17,16,128]{2,1,0:T(8,128)(2,1)S(1)} %add_convert_fusion.2), channel_id=1, source_target_pairs={{0,2},{1,3},{2,0},{3,1},{4,6},{5,7},{6,4},{7,5},{8,10},{9,11},{10,... | collective-permute-start | bytes 208904 | tf_op jit(solution)/shard_map/ppermute | solution.py:282
  17.0 5.2 %collective-permute-start.3 = (bf16[17,16,128]{2,1,0:T(8,128)(2,1)S(1)}, bf16[17,16,128]{2,1,0:T(8,128)(2,1)S(1)}, u32[]{:S(2)}, u32[]{:S(2)}) collective-permute-start(bf16[17,16,128]{2,1,0:T(8,128)(2,1)S(1)} %add_convert_fusion.2), channel_id=1, source_target_pairs={{0,16},{1,17},{2,18},{3,19},{4,20},{5,21},{6,22},{7,23},{8,24},{9,... | collective-permute-start | bytes 208904 | tf_op jit(solution)/shard_map/ppermute | solution.py:282
  20.8 1.5 %collective-permute-start.7 = (bf16[17,16,128]{2,1,0:T(8,128)(2,1)S(1)}, bf16[17,16,128]{2,1,0:T(8,128)(2,1)S(1)}, u32[]{:S(2)}, u32[]{:S(2)}) collective-permute-start(bf16[17,16,128]{2,1,0:T(8,128)(2,1)S(1)} %add_convert_fusion.refs_2_), channel_id=1, source_target_pairs={{0,1},{1,0},{2,3},{3,2},{4,5},{5,4},{6,7},{7,6},{8,9},{9,8},{10,11... | collective-permute-start | bytes 208904 | tf_op jit(solution)/shard_map/ppermute | solution.py:282
  22.2 1.3 %collective-permute-start.4 = (bf16[17,16,128]{2,1,0:T(8,128)(2,1)S(1)}, bf16[17,16,128]{2,1,0:T(8,128)(2,1)S(1)}, u32[]{:S(2)}, u32[]{:S(2)}) collective-permute-start(bf16[17,16,128]{2,1,0:T(8,128)(2,1)S(1)} %add_convert_fusion.1.refs_0_), channel_id=1, source_target_pairs={{0,1},{1,0},{2,3},{3,2},{4,5},{5,4},{6,7},{7,6},{8,9},{9,8},{10,11... | collective-permute-start | bytes 208904 | tf_op jit(solution)/shard_map/ppermute | solution.py:282
  24.1 4.3 %collective-permute-start.10 = (f32[64,128]{1,0:T(8,128)S(1)}, f32[64,128]{1,0:T(8,128)S(1)}, u32[]{:S(2)}, u32[]{:S(2)}) collective-permute-start(f32[64,128]{1,0:T(8,128)S(1)} %get-tuple-element.15.m0), channel_id=1, source_target_pairs={{0,13},{1,12},{2,15},{3,14},{4,9},{5,8},{6,11},{7,10},{8,5},{9,4},... | collective-permute-start | bytes 98312 | tf_op jit(solution)/shard_map/ppermute | solution.py:282
  25.4 3.3 %collective-permute-start.9 = (f32[64,128]{1,0:T(8,128)S(1)}, f32[64,128]{1,0:T(8,128)S(1)}, u32[]{:S(2)}, u32[]{:S(2)}) collective-permute-start(f32[64,128]{1,0:T(8,128)S(1)} %get-tuple-element.15.m0), channel_id=1, source_target_pairs={{0,9},{1,8},{2,11},{3,10},{4,13},{5,12},{6,15},{7,14},{8,1},{9,0},... | collective-permute-start | bytes 98312 | tf_op jit(solution)/shard_map/ppermute | solution.py:282
  26.0 3.3 %collective-permute-start.8 = (f32[64,128]{1,0:T(8,128)S(1)}, f32[64,128]{1,0:T(8,128)S(1)}, u32[]{:S(2)}, u32[]{:S(2)}) collective-permute-start(f32[64,128]{1,0:T(8,128)S(1)} %get-tuple-element.15.m0), channel_id=1, source_target_pairs={{0,5},{1,4},{2,7},{3,6},{4,1},{5,0},{6,3},{7,2},{8,13},{9,12},{10,... | collective-permute-start | bytes 98312 | tf_op jit(solution)/shard_map/ppermute | solution.py:282
